TPU v7x, 32 devices: a whole 2x2x4 slice. The times are simulated.
32 devices in a mesh: lat: 8 (over y, x, core), lon: 4 (over z).
Axes of the slice: x: 2, y: 2, z: 4, core: 2. Of those that a mesh axis runs over, the one named last changes fastest.
Arguments:
- fields: bfloat16 [256, 128, 256], P('lat', 'lon'), may hold values from -6 to 6
- w_conv1: bfloat16 [3, 3, 256, 256], replicated, may hold values from -0.125 to 0.125
- b_conv1: float32 [256], replicated, may hold values from -3 to 3
- w_conv2: bfloat16 [3, 3, 256, 256], replicated, may hold values from -0.125 to 0.125
- b_conv2: float32 [256], replicated, may hold values from -3 to 3
- w_query: bfloat16 [256, 256], replicated, may hold values from -16 to 16
- w_key: bfloat16 [256, 64], replicated, may hold values from -1 to 1
- w_value: bfloat16 [256, 64], replicated, may hold values from -0.375 to 0.375
- w_out: bfloat16 [256, 256], replicated, may hold values from -0.375 to 0.375
- rotation: int32 [8, 4], replicated, may hold values from 0 to 3
- owner: int32 [8, 4], replicated, may hold values from 0 to 3, as said below
- counts: int32 [256], replicated, may hold values from 4 to 128
Outputs:
- fields_out: bfloat16 [256, 128, 256], P('lat', 'lon')
Inputs may be any that keep to these rules, and one draw needn't show every extreme that they name: Each row of owner holds every number from 0 to 3 exactly once.
All inputs are finite; a program needn't handle non-finite values.
Results may differ from a plain program's by a relative error of at most 0.014.
Values may be sent and summed in bfloat16 or wider, within the bound.
No kernel may reach another device: no remote copies, remote signals or barrier semaphores. Data moves between devices by JAX's collectives and lax.ppermute only.
A program may use at most 64 MiB of HBM per device.

v0:
```python
import math

import jax
import jax.numpy as jnp
from jax import lax
from jax.sharding import PartitionSpec as P


def shortened(x):

    def short(part):
        return part.astype(jnp.bfloat16) if part.dtype == jnp.float32 else part

    return jax.tree.map(short, x)


def passed_along(x, axis, by):
    devices = lax.axis_size(axis)
    pairs = [(i, i + by) for i in range(devices) if 0 <= i + by < devices]
    return lax.ppermute(x, axis, pairs)


def turn_block(block, quarter_turns):
    options = [lambda m, k=k: jnp.rot90(m, k, axes=(0, 1)) for k in range(4)]
    return lax.switch(quarter_turns % 4, options, block)


def inverse_owner(owner):
    shards = jnp.arange(owner.shape[1], dtype=jnp.int32)
    matches = owner[:, None, :] == shards[None, :, None]
    return jnp.sum(jnp.where(matches, shards[None, None, :], 0), axis=2)


def live_region(counts, first_row, row_count, first_col, col_count, total_cols):
    padded_counts = jnp.pad(counts, 2)
    row_limits = lax.dynamic_slice_in_dim(padded_counts, first_row + 2, row_count)
    columns = (first_col + jnp.arange(col_count, dtype=jnp.int32)) % total_cols
    return (columns[None, :] < row_limits[:, None]).astype(jnp.float32)


def pick_block(stack, inverse, band_row, segment):
    return lax.dynamic_index_in_dim(stack, inverse[band_row, segment], 0, keepdims=False)


def fetch_halo(part, width, inverse, band_index, segment):
    lat_size = lax.axis_size("lat")
    lon_size = lax.axis_size("lon")
    block_size = part.shape[0]
    chans = part.shape[2]
    from_north = passed_along(shortened(part[-width:]), "lat", 1)
    from_south = passed_along(shortened(part[:width]), "lat", -1)
    west_all, east_all, north_all, south_all = (
        lax.all_gather(shortened(part[:, :width]), "lon", axis=0, tiled=True),
        lax.all_gather(shortened(part[:, -width:]), "lon", axis=0, tiled=True),
        lax.all_gather(shortened(from_north), "lon", axis=0, tiled=True).astype(from_north.dtype),
        lax.all_gather(shortened(from_south), "lon", axis=0, tiled=True).astype(from_south.dtype),
    )
    west_all = west_all.reshape(lon_size, block_size, width, chans)
    east_all = east_all.reshape(lon_size, block_size, width, chans)
    north_all = north_all.reshape(lon_size, width, block_size, chans)
    south_all = south_all.reshape(lon_size, width, block_size, chans)
    west_segment = (segment - 1) % lon_size
    east_segment = (segment + 1) % lon_size
    north_band = jnp.maximum(band_index - 1, 0)
    south_band = jnp.minimum(band_index + 1, lat_size - 1)
    left_cols = pick_block(east_all, inverse, band_index, west_segment)
    right_cols = pick_block(west_all, inverse, band_index, east_segment)
    upper = jnp.concatenate(
        [
            pick_block(north_all, inverse, north_band, west_segment)[:, -width:],
            pick_block(north_all, inverse, north_band, segment),
            pick_block(north_all, inverse, north_band, east_segment)[:, :width],
        ],
        axis=1,
    )
    lower = jnp.concatenate(
        [
            pick_block(south_all, inverse, south_band, west_segment)[:, -width:],
            pick_block(south_all, inverse, south_band, segment),
            pick_block(south_all, inverse, south_band, east_segment)[:, :width],
        ],
        axis=1,
    )
    middle = jnp.concatenate([left_cols, part, right_cols], axis=1)
    return jnp.concatenate([upper, middle, lower], axis=0)


def convolve(padded, weight, bias, out_rows, out_cols):
    chans = padded.shape[2]
    total = jnp.zeros((out_rows * out_cols, chans), jnp.float32) + bias
    for i in range(3):
        for j in range(3):
            window = padded[i : i + out_rows, j : j + out_cols].reshape(out_rows * out_cols, chans)
            total = total + jnp.dot(window, weight[i, j], preferred_element_type=jnp.float32)
    return total.reshape(out_rows, out_cols, chans)


def on_device(
    fields,
    w_conv1,
    b_conv1,
    w_conv2,
    b_conv2,
    w_query,
    w_key,
    w_value,
    w_out,
    rotation,
    owner,
    counts,
):
    block_size = fields.shape[0]
    chans = fields.shape[2]
    head_dim = w_key.shape[1]
    heads = chans // head_dim
    lon_size = lax.axis_size("lon")
    band_index = lax.axis_index("lat")
    shard_index = lax.axis_index("lon")
    quarter = rotation[band_index, shard_index]
    segment = owner[band_index, shard_index]
    owner_row = owner[band_index]
    inverse = inverse_owner(owner)
    upright = turn_block(fields, (4 - quarter) % 4)
    total_cols = block_size * lon_size
    first_row = band_index * block_size
    first_col = segment * block_size
    live_own = live_region(counts, first_row, block_size, first_col, block_size, total_cols)[
        :, :, None
    ]
    padded = fetch_halo(upright, 1, inverse, band_index, segment)
    first = convolve(padded, w_conv1, b_conv1, block_size, block_size)
    act = (jax.nn.silu(first) * live_own).astype(jnp.bfloat16)
    act_padded = fetch_halo(act, 1, inverse, band_index, segment)
    second = convolve(act_padded, w_conv2, b_conv2, block_size, block_size)
    mixed = ((upright.astype(jnp.float32) + second) * live_own).astype(jnp.bfloat16)
    flat = mixed.reshape(block_size * block_size, chans).astype(jnp.float32)
    normed = (flat * lax.rsqrt(jnp.mean(flat * flat, axis=1, keepdims=True) + 1e-06)).astype(
        jnp.bfloat16
    )
    query = jnp.dot(normed, w_query, preferred_element_type=jnp.float32).astype(jnp.bfloat16)
    query = query.reshape(block_size, block_size, chans)
    key_val = jnp.dot(
        normed, jnp.concatenate([w_key, w_value], axis=1), preferred_element_type=jnp.float32
    )
    key_val = key_val.astype(jnp.bfloat16).reshape(block_size, block_size, 2 * head_dim)
    root_dim = math.sqrt(head_dim)
    heads_q = query.reshape(block_size, block_size, heads, head_dim)
    row_limits = lax.dynamic_slice_in_dim(counts, first_row, block_size)
    piece = lax.all_gather(key_val, "lon", axis=1, tiled=True)
    summed = jnp.zeros((block_size, block_size, heads, head_dim), jnp.float32)
    peak = jnp.full((block_size, block_size, heads), -jnp.inf, jnp.float32)
    total = jnp.zeros((block_size, block_size, heads), jnp.float32)
    positions = jnp.arange(piece.shape[1], dtype=jnp.int32)
    true_cols = owner_row[positions // block_size] * block_size + positions % block_size
    live_keys = true_cols[None, :] < row_limits[:, None]
    scores = (
        jnp.einsum(
            "rchd,rkd->rchk", heads_q, piece[:, :, :head_dim], preferred_element_type=jnp.float32
        )
        / root_dim
    )
    scores = jnp.where(live_keys[:, None, None, :], scores, -jnp.inf)
    new_peak = jnp.max(scores, axis=3)
    safe_peak = jnp.where(jnp.isfinite(new_peak), new_peak, 0.0)
    expo = jnp.exp(scores - safe_peak[..., None])
    shrink = jnp.exp(peak - safe_peak)
    total = total * shrink + jnp.sum(expo, axis=3)
    summed = summed * shrink[..., None] + jnp.einsum(
        "rchk,rkd->rchd",
        expo.astype(jnp.bfloat16),
        piece[:, :, head_dim:],
        preferred_element_type=jnp.float32,
    )
    summed, peak, total = (summed, new_peak, total)
    attended = (
        (summed / total[..., None]).astype(jnp.bfloat16).reshape(block_size * block_size, chans)
    )
    update = jnp.dot(attended, w_out, preferred_element_type=jnp.float32).reshape(
        block_size, block_size, chans
    )
    result = (mixed.astype(jnp.float32) + update * live_own).astype(jnp.bfloat16)
    return turn_block(result, quarter)


def solution(mesh):
    in_specs = (P("lat", "lon", None), P(), P(), P(), P(), P(), P(), P(), P(), P(), P(), P())
    out_specs = P("lat", "lon", None)
    return jax.shard_map(
        on_device, mesh=mesh, in_specs=in_specs, out_specs=out_specs, check_vma=False
    )
```

profile of v0, /device:TPU:0, one launch (start us, length us, event | category | flops | bytes accessed | tf_op | source)
XLA Modules:
  0.0 212.9 jit_solution(4827806496707147337)
XLA Ops:
  6.5 1.3 dynamic_slice.73
  8.6 1.2 conditional.2
  8.6 1.2 rev.20
  10.1 1.3 collective-permute-start.1
  11.4 3.0 %collective-permute-start = (bf16[1,32,256]{2,1,0:T(8,128)(2,1)S(1)}, bf16[1,32,256]{2,1,0:T(8,128)(2,1)S(1)}, u32[]{:S(2)}, u32[]{:S(2)}) collective-permute-start(bf16[1,32,256]{2,1,0:T(8,128)(2,1)S(1)} %get-tuple-element.52), channel_id=1, source_target_pairs={{0,4},{4,8},{8,12},{12,16},{16,20},{20,24},{24,28},{1,5},{5,9},{9,... | collective-permute-start | bytes 49160 | tf_op jit(solution)/shard_map/ppermute | solution.py:20
  22.5 14.9 %all_gather.29 = bf16[128,1,256]{2,0,1:T(8,128)(2,1)S(1)} all-gather(bf16[32,1,256]{2,0,1:T(8,128)(2,1)S(1)} %get-tuple-element.56), channel_id=1, replica_groups=mesh['lat'=8,'lon'=4] {'lon'}, dimensions={0}, use_global_device_ids=true | all-gather | bytes 81920 | tf_op jit(solution)/shard_map/all_gather | solution.py:53
  38.1 13.1 %all_gather.28 = bf16[128,1,256]{2,0,1:T(8,128)(2,1)S(1)} all-gather(bf16[32,1,256]{2,0,1:T(8,128)(2,1)S(1)} %get-tuple-element.55), channel_id=1, replica_groups=mesh['lat'=8,'lon'=4] {'lon'}, dimensions={0}, use_global_device_ids=true | all-gather | bytes 81920 | tf_op jit(solution)/shard_map/all_gather | solution.py:54
  64.0 13.2 %all_gather.30 = bf16[4,32,256]{2,1,0:T(8,128)(2,1)S(1)} all-gather(bf16[1,32,256]{2,1,0:T(8,128)(2,1)S(1)} %collective-permute-done.1), channel_id=1, replica_groups=mesh['lat'=8,'lon'=4] {'lon'}, dimensions={0}, use_global_device_ids=true | all-gather | bytes 81920 | tf_op jit(solution)/shard_map/all_gather | solution.py:56
  77.2 13.2 %all_gather.27 = bf16[4,32,256]{2,1,0:T(8,128)(2,1)S(1)} all-gather(bf16[1,32,256]{2,1,0:T(8,128)(2,1)S(1)} %collective-permute-done), channel_id=1, replica_groups=mesh['lat'=8,'lon'=4] {'lon'}, dimensions={0}, use_global_device_ids=true | all-gather | bytes 81920 | tf_op jit(solution)/shard_map/all_gather | solution.py:55
  95.3 1.3 collective-permute-start.3
  96.6 13.2 %all_gather.33 = bf16[128,1,256]{2,0,1:T(8,128)(2,1)S(1)} all-gather(bf16[32,1,256]{2,0,1:T(8,128)(2,1)S(1)} %copy.118), channel_id=1, replica_groups=mesh['lat'=8,'lon'=4] {'lon'}, dimensions={0}, use_global_device_ids=true | all-gather | bytes 81920 | tf_op jit(solution)/shard_map/all_gather | solution.py:53
  109.8 13.2 %all_gather.32 = bf16[128,1,256]{2,0,1:T(8,128)(2,1)S(1)} all-gather(bf16[32,1,256]{2,0,1:T(8,128)(2,1)S(1)} %copy.117), channel_id=1, replica_groups=mesh['lat'=8,'lon'=4] {'lon'}, dimensions={0}, use_global_device_ids=true | all-gather | bytes 81920 | tf_op jit(solution)/shard_map/all_gather | solution.py:54
  123.1 1.3 collective-permute-start.2
  124.8 13.3 %all_gather.34 = bf16[4,32,256]{2,1,0:T(8,128)(2,1)S(1)} all-gather(bf16[1,32,256]{2,1,0:T(8,128)(2,1)S(1)} %collective-permute-done.3), channel_id=1, replica_groups=mesh['lat'=8,'lon'=4] {'lon'}, dimensions={0}, use_global_device_ids=true | all-gather | bytes 81920 | tf_op jit(solution)/shard_map/all_gather | solution.py:56
  138.2 13.3 %all_gather.31 = bf16[4,32,256]{2,1,0:T(8,128)(2,1)S(1)} all-gather(bf16[1,32,256]{2,1,0:T(8,128)(2,1)S(1)} %collective-permute-done.2), channel_id=1, replica_groups=mesh['lat'=8,'lon'=4] {'lon'}, dimensions={0}, use_global_device_ids=true | all-gather | bytes 81920 | tf_op jit(solution)/shard_map/all_gather | solution.py:55
  161.5 2.4 %fusion.58 = s32[128]{0:T(128)S(1)} fusion(s32[]{:T(128)} %bitcast.59, s32[]{:T(128)} %bitcast.60, s32[]{:T(128)} %bitcast.62, s32[]{:T(128)} %bitcast.61), kind=kLoop, calls=%fused_computation.133 | loop fusion | flops 3200 | bytes 528 | tf_op jit(solution)/shard_map/add | solution.py:154
  164.3 1.4 reshape_reshape.3
  165.6 23.6 %all-gather.2.cloned.1.call-done = bf16[32,128,128]{2,0,1:T(8,128)(2,1)} async-done(((bf16[32,32,128]{2,0,1:T(8,128)(2,1)}), bf16[32,128,128]{2,0,1:T(8,128)(2,1)}) %all-gather.2.cloned.1.call-update) | async-done | bytes 1048592 | tf_op jit(solution)/shard_map/all_gather | solution.py:149
  189.2 3.0 %fusion.68 = (bf16[32,128,64]{2,0,1:T(8,128)(2,1)S(1)}, bf16[32,128,64]{2,0,1:T(8,128)(2,1)}) fusion(bf16[32,128,128]{2,0,1:T(8,128)(2,1)} %all-gather.2.cloned.1.call-done), kind=kLoop, calls=%fused_computation.142 | loop fusion | bytes 2097152 | tf_op jit(solution)/shard_map/slice | solution.py:171
  192.1 2.2 %copy.137 = bf16[32,128,64]{1,2,0:T(8,128)(2,1)S(1)} copy(bf16[32,128,64]{2,0,1:T(8,128)(2,1)} %get-tuple-element.28) | data formatting | bytes 1048576
  194.4 2.0 fusion
  196.4 1.3 copy-done.2
  197.8 1.4 fusion.1
  200.3 3.0 %divide_convert_fusion = bf16[32,32,4,64]{3,1,2,0:T(8,128)(2,1)S(1)} fusion(f32[32,32,4,128]{3,1,2,0:T(8,128)} %copy-done.2, f32[32,32,4]{1,2,0:T(4,128)S(1)} %get-tuple-element.58, f32[32,32,4]{1,2,0:T(4,128)S(1)} %is-finite_select_fusion, f32[32,32,4]{1,2,0:T(4,128)S(1)} %get-tuple-element.57, pred[32,128]{1,0:T(8,128)(4,1)S(1)} %broadcast_compare_fusion, ...), kind=kOutput, calls=%fused_computation | convolution fusion | flops 69992448 | bytes 3198976 | tf_op jit(solution)/shard_map/rchk,rkd->rchd/dot_general | solution.py:168
  (107 shorter events, 20.4 us)
Async XLA Ops:
  6.5 157.4 %copy-start = (bf16[256,256]{1,0:T(8,128)(2,1)S(1)}, bf16[256,256]{1,0:T(8,128)(2,1)}, u32[]{:S(2)}) copy-start(bf16[256,256]{1,0:T(8,128)(2,1)} %param.25) | copy-start | bytes 393220
  6.5 182.6 %all-gather.2.cloned.1.call-start = ((), (), s32[]{:S(2)}) async-start(), calls=%async_computation | async-start | bytes 1310720 | tf_op jit(solution)/shard_map/all_gather | solution.py:149
  8.5 5.9 %copy-start.8 = (s32[8,4]{0,1:T(4,128)S(1)}, s32[8,4]{0,1:T(4,128)}, u32[]{:S(2)}) copy-start(s32[8,4]{0,1:T(4,128)} %param.30) | copy-start | bytes 388
  8.6 13.8 %copy-start.9 = (s32[256]{0:T(256)S(1)}, s32[256]{0:T(256)}, u32[]{:S(2)}) copy-start(s32[256]{0:T(256)} %param.31) | copy-start | bytes 3076
  10.1 53.9 %collective-permute-start.1 = (bf16[1,32,256]{2,1,0:T(8,128)(2,1)S(1)}, bf16[1,32,256]{2,1,0:T(8,128)(2,1)S(1)}, u32[]{:S(2)}, u32[]{:S(2)}) collective-permute-start(bf16[1,32,256]{2,1,0:T(8,128)(2,1)S(1)} %get-tuple-element.51), channel_id=1, source_target_pairs={{4,0},{8,4},{12,8},{16,12},{20,16},{24,20},{28,24},{5,1},{9,5},{13... | collective-permute-start | bytes 49160 | tf_op jit(solution)/shard_map/ppermute | solution.py:20
  11.4 65.8 %collective-permute-start = (bf16[1,32,256]{2,1,0:T(8,128)(2,1)S(1)}, bf16[1,32,256]{2,1,0:T(8,128)(2,1)S(1)}, u32[]{:S(2)}, u32[]{:S(2)}) collective-permute-start(bf16[1,32,256]{2,1,0:T(8,128)(2,1)S(1)} %get-tuple-element.52), channel_id=1, source_target_pairs={{0,4},{4,8},{8,12},{12,16},{16,20},{20,24},{24,28},{1,5},{5,9},{9,... | collective-permute-start | bytes 49160 | tf_op jit(solution)/shard_map/ppermute | solution.py:20
  90.9 1.3 copy-start.3
  91.0 1.3 copy-start.10
  95.3 29.5 %collective-permute-start.3 = (bf16[1,32,256]{2,1,0:T(8,128)(2,1)S(1)}, bf16[1,32,256]{2,1,0:T(8,128)(2,1)S(1)}, u32[]{:S(2)}, u32[]{:S(2)}) collective-permute-start(bf16[1,32,256]{2,1,0:T(8,128)(2,1)S(1)} %get-tuple-element.45), channel_id=1, source_target_pairs={{4,0},{8,4},{12,8},{16,12},{20,16},{24,20},{28,24},{5,1},{9,5},{13... | collective-permute-start | bytes 49160 | tf_op jit(solution)/shard_map/ppermute | solution.py:20
  123.1 15.1 %collective-permute-start.2 = (bf16[1,32,256]{2,1,0:T(8,128)(2,1)S(1)}, bf16[1,32,256]{2,1,0:T(8,128)(2,1)S(1)}, u32[]{:S(2)}, u32[]{:S(2)}) collective-permute-start(bf16[1,32,256]{2,1,0:T(8,128)(2,1)S(1)} %get-tuple-element.46), channel_id=1, source_target_pairs={{0,4},{4,8},{8,12},{12,16},{16,20},{20,24},{24,28},{1,5},{5,9},{9,... | collective-permute-start | bytes 49160 | tf_op jit(solution)/shard_map/ppermute | solution.py:20
  152.4 1.3 copy-start.4
  152.4 1.3 copy-start.11
  157.0 0.8 copy-start.6
  157.1 0.8 copy-start.7
  196.4 1.3 copy-start.2
  203.3 1.2 copy-start.5
  205.3 0.8 copy-start.1
Sparse Core Ops, SparseCore 0:
  159.1 30.0 all-gather.1
where the time goes:
time: 214 us; the launch traced here: 213 us
  blocking collectives  107 us (50%)
  between operations  35.7 us (17%)
  waiting for transfers between devices  23.6 us (11%)
  local copies, waits for them, and re-layouts  20.8 us (10%)
  matrix products  11.4 us (5%)
  other arithmetic  6.97 us (3%)
  starting transfers between devices  6.91 us (3%)
    all_gather x2, blocking collectives, fetch_halo(): lax.all_gather(shortened(part[:, :width]), 'lon', axis=0, tiled=True)  28.1 us
    all_gather x2, blocking collectives, fetch_halo(): lax.all_gather(shortened(from_south), 'lon', axis=0, tiled=True)  26.5 us
    all_gather x2, blocking collectives, fetch_halo(): lax.all_gather(shortened(from_north), 'lon', axis=0, tiled=True)  26.5 us
    all_gather x2, blocking collectives, fetch_halo(): lax.all_gather(shortened(part[:, -width:]), 'lon', axis=0, tiled=True)  26.3 us
    all_gather x1, waiting for transfers between devices, on_device(): piece = lax.all_gather(key_val, 'lon', axis=1, tiled=True)  23.6 us
    unnamed x26, local copies, waits for them, and re-layouts  7.29 us
    ppermute x4, starting transfers between devices, passed_along(): return lax.ppermute(x, axis, pairs)  6.91 us
    dot_general x18, matrix products, convolve(): jnp.dot(window, weight[i, j], preferred_element_type=jnp.float32)  5.48 us
  transfers between devices with their start and end apart: 5, of which 1 were waited for; matrix products, arithmetic and copies ran while one was open for 4% of the time, Pallas kernels for 0%

commit v1 on v0

v1 whole, which is shorter than its diff:
```python
import functools

import jax
import jax.numpy as jnp
from jax import lax
from jax.experimental import pallas as pl
from jax.experimental.pallas import tpu as pltpu
from jax.sharding import PartitionSpec as P

HALO = 2
LANES = 128
VMEM_BYTES = 48 * 1024 * 1024


def turn(quarter, size, staged, spare, load_row, store_row):
    tiles = staged.shape[0]

    def column(ref, col):
        parts = [ref[t, pl.ds(col, size, stride=size), :] for t in range(tiles)]
        return jnp.concatenate(parts, axis=1)

    def keep(ref, i, row):
        for t in range(tiles):
            ref[t, pl.ds(i * size, size), :] = row[:, t * LANES : (t + 1) * LANES]

    @pl.when(quarter == 0)
    def _():
        for i in range(size):
            store_row(i, load_row(i))

    @pl.when(quarter == 1)
    def _():
        for i in range(size):
            keep(staged, i, load_row(i).astype(jnp.float32))
        for i in range(size):
            store_row(i, column(staged, size - 1 - i).astype(jnp.bfloat16))

    @pl.when(quarter == 2)
    def _():
        for i in range(size):
            keep(staged, i, load_row(i).astype(jnp.float32))
        for i in range(size):
            keep(spare, i, column(staged, size - 1 - i))
        for i in range(size):
            store_row(i, column(spare, size - 1 - i).astype(jnp.bfloat16))

    @pl.when(quarter == 3)
    def _():
        for i in range(size):
            keep(staged, size - 1 - i, load_row(i).astype(jnp.float32))
        for i in range(size):
            store_row(i, column(staged, i).astype(jnp.bfloat16))


def send_kernel(n, rows, rotation, fields, *rest):
    slabs, edges = rest[:n], rest[n : 2 * n]
    staged, spare, upright = rest[2 * n :]
    size = fields.shape[0]
    me = lax.axis_index("lon")
    quarter = rotation[lax.axis_index("lat"), me]
    blank = jnp.zeros((HALO,) + upright.shape[1:], upright.dtype)
    upright[:HALO] = blank
    upright[HALO + size :] = blank

    def store_row(i, row):
        upright[HALO + i] = row

    turn((4 - quarter) % 4, size, staged, spare, lambda i: fields[i], store_row)
    for d in range(n):
        to = lax.rem(me + d, n)
        slabs[d][...] = upright[pl.ds(to * rows, rows + 2 * HALO)]
    for k in range(n):
        edges[k][...] = upright[pl.ds(jnp.where(me == k, size, HALO), HALO)]


def row_kernel(n, rows, owner, counts, *rest):
    slabs, edges = rest[:n], rest[n : 2 * n]
    w_conv1, b_conv1, w_conv2, b_conv2, w_query, w_kv, w_out = rest[2 * n : 2 * n + 7]
    results = rest[2 * n + 7 : 3 * n + 7]
    taps1, taps2 = rest[3 * n + 7 :]
    band = lax.axis_index("lat")
    me = lax.axis_index("lon")
    bands = owner.shape[0]
    size, chans = slabs[0].shape[1:]
    cols = size * n
    centre = slice(chans, 2 * chans)

    def columns_of(segment):
        return pl.ds(pl.multiple_of(segment * size, size), size)

    for d in range(n):
        source = lax.rem(me + n - d, n)
        taps1[:, columns_of(owner[band, source]), centre] = slabs[d][...]

    @pl.when(me == 0)
    def _():
        north = jnp.maximum(band - 1, 0)
        for k in range(n):
            taps1[:HALO, columns_of(owner[north, k]), centre] = edges[k][...]

    @pl.when(me == n - 1)
    def _():
        south = jnp.minimum(band + 1, bands - 1)
        for k in range(n):
            taps1[rows + HALO :, columns_of(owner[south, (k + 1) % n]), centre] = edges[k][...]

    def spread(taps, r):
        row = taps[r, :, centre].astype(jnp.float32)
        taps[r, :, :chans] = pltpu.roll(row, 1, 0).astype(jnp.bfloat16)
        taps[r, :, 2 * chans :] = pltpu.roll(row, cols - 1, 0).astype(jnp.bfloat16)

    def convolve(taps, weight, bias, count):
        total = bias[...]
        for i in range(3):
            window = taps[i : i + count].reshape(count * cols, 3 * chans)
            total = total + jnp.dot(window, weight[i], preferred_element_type=jnp.float32)
        return total

    def live_count(row):
        inside = (row >= 0) & (row < bands * size)
        return jnp.where(inside, counts[jnp.clip(row, 0, bands * size - 1)], 0)

    cell = lax.broadcasted_iota(jnp.int32, (cols, chans), 0)
    first_row = band * size + me * rows

    for r in range(rows + 2 * HALO):
        spread(taps1, r)
    first = convolve(taps1, w_conv1, b_conv1, rows + 2)
    silu = first / (1.0 + jnp.exp(-first))
    for r in range(rows + 2):
        live = cell < live_count(first_row + r - 1)
        act = jnp.where(live, silu[r * cols : (r + 1) * cols], 0.0)
        taps2[r, :, centre] = act.astype(jnp.bfloat16)
        spread(taps2, r)
    second = convolve(taps2, w_conv2, b_conv2, rows)

    head_dim = 64
    heads = chans // head_dim
    lane_head = lax.broadcasted_iota(jnp.int32, (cols, chans), 1) // head_dim
    key_at = lax.broadcasted_iota(jnp.int32, (cols, heads * cols), 1) % cols

    def per_head(x):
        return jnp.concatenate([jnp.where(lane_head == h, x, jnp.zeros_like(x)) for h in range(heads)], axis=0)

    ones = per_head(jnp.ones((cols, chans), jnp.bfloat16))
    for r in range(rows):
        count = counts[first_row + r]
        live = cell < count
        grid = taps1[r + HALO, :, centre].astype(jnp.float32)
        mixed = jnp.where(live, grid + second[r * cols : (r + 1) * cols], 0.0).astype(jnp.bfloat16)
        flat = mixed.astype(jnp.float32)
        normed = (flat * lax.rsqrt(jnp.mean(flat * flat, axis=1, keepdims=True) + 1e-06)).astype(jnp.bfloat16)
        query = jnp.dot(normed, w_query[...], preferred_element_type=jnp.float32).astype(jnp.bfloat16)
        key_val = jnp.dot(normed, w_kv[...], preferred_element_type=jnp.float32).astype(jnp.bfloat16)
        keys = per_head(key_val[:, :chans])
        values = per_head(key_val[:, chans:])
        scores = lax.dot_general(query, keys, (((1,), (1,)), ((), ())), preferred_element_type=jnp.float32)
        scores = jnp.where(key_at < count, scores * (1.0 / head_dim**0.5), -jnp.inf)
        expo = []
        for h in range(heads):
            part = scores[:, h * cols : (h + 1) * cols]
            expo.append(jnp.exp(part - jnp.max(part, axis=1, keepdims=True)))
        weights = jnp.concatenate(expo, axis=1).astype(jnp.bfloat16)
        summed = jnp.dot(weights, values, preferred_element_type=jnp.float32)
        total = jnp.dot(weights, ones, preferred_element_type=jnp.float32)
        attended = (summed / total).astype(jnp.bfloat16)
        update = jnp.dot(attended, w_out[...], preferred_element_type=jnp.float32)
        taps2[r, :, centre] = (flat + jnp.where(live, update, 0.0)).astype(jnp.bfloat16)
    for d in range(n):
        to = lax.rem(me + d, n)
        results[d][...] = taps2[:rows, columns_of(owner[band, to]), centre]


def store_kernel(n, rows, rotation, *rest):
    slabs = rest[:n]
    out, staged, spare, upright = rest[n:]
    size = out.shape[0]
    me = lax.axis_index("lon")
    quarter = rotation[lax.axis_index("lat"), me]
    for d in range(n):
        source = lax.rem(me + n - d, n)
        upright[pl.ds(source * rows, rows)] = slabs[d][...]

    def store_row(i, row):
        out[i] = row

    turn(quarter % 4, size, staged, spare, lambda i: upright[i], store_row)


def on_device(
    bands,
    n,
    fields,
    w_conv1,
    b_conv1,
    w_conv2,
    b_conv2,
    w_query,
    w_key,
    w_value,
    w_out,
    rotation,
    owner,
    counts,
):
    size, _, chans = fields.shape
    rows = size // n
    cols = size * n
    heads = chans // w_key.shape[1]
    smem = pl.BlockSpec(memory_space=pltpu.SMEM)
    vmem = pl.BlockSpec(memory_space=pltpu.VMEM)
    params = pltpu.CompilerParams(vmem_limit_bytes=VMEM_BYTES)
    bf16 = jnp.bfloat16
    slab = jax.ShapeDtypeStruct((rows + 2 * HALO, size, chans), bf16)
    edge = jax.ShapeDtypeStruct((HALO, size, chans), bf16)
    piece = jax.ShapeDtypeStruct((rows, size, chans), bf16)
    staging = [pltpu.VMEM((chans // LANES, size * size, LANES), jnp.float32)] * 2

    sent = pl.pallas_call(
        functools.partial(send_kernel, n, rows),
        out_shape=[slab] * n + [edge] * n,
        in_specs=[smem, vmem],
        out_specs=[vmem] * (2 * n),
        scratch_shapes=staging + [pltpu.VMEM((size + 2 * HALO, size, chans), bf16)],
        compiler_params=params,
        name="send",
    )(rotation, fields)

    def around(x, d):
        return lax.ppermute(x, "lon", [(i, (i + d) % n) for i in range(n)])

    slabs = [sent[0]] + [around(sent[d], d) for d in range(1, n)]
    edges = []
    for k in range(n):
        pairs = [(a * n + k, (a + 1) * n) for a in range(bands - 1)]
        pairs += [(a * n + (k + 1) % n, a * n - 1) for a in range(1, bands)]
        edges.append(lax.ppermute(sent[n + k], ("lat", "lon"), pairs))

    w_kv = jnp.concatenate([w_key] * heads + [w_value] * heads, axis=1)
    results = pl.pallas_call(
        functools.partial(row_kernel, n, rows),
        out_shape=[piece] * n,
        in_specs=[smem] * 2 + [vmem] * (2 * n + 7),
        out_specs=[vmem] * n,
        scratch_shapes=[
            pltpu.VMEM((rows + 2 * HALO, cols, 3 * chans), bf16),
            pltpu.VMEM((rows + 2, cols, 3 * chans), bf16),
        ],
        compiler_params=params,
        name="rows",
    )(
        owner,
        counts,
        *slabs,
        *edges,
        w_conv1.reshape(3, 3 * chans, chans),
        b_conv1.reshape(1, chans),
        w_conv2.reshape(3, 3 * chans, chans),
        b_conv2.reshape(1, chans),
        w_query,
        w_kv,
        w_out,
    )
    back = [results[0]] + [around(results[d], d) for d in range(1, n)]
    return pl.pallas_call(
        functools.partial(store_kernel, n, rows),
        out_shape=jax.ShapeDtypeStruct(fields.shape, bf16),
        in_specs=[smem] + [vmem] * n,
        out_specs=vmem,
        scratch_shapes=staging + [pltpu.VMEM((size, size, chans), bf16)],
        compiler_params=params,
        name="store",
    )(rotation, *back)


def solution(mesh):
    in_specs = (P("lat", "lon", None), P(), P(), P(), P(), P(), P(), P(), P(), P(), P(), P())
    out_specs = P("lat", "lon", None)
    body = functools.partial(on_device, mesh.shape["lat"], mesh.shape["lon"])
    return jax.shard_map(body, mesh=mesh, in_specs=in_specs, out_specs=out_specs, check_vma=False)
```

time: 214 us -> 65 us (0.30)
  the two profiles are of different devices: /device:TPU:0 before, /device:TPU:12 now
where the time goes in v1:
time: 65 us; the launch traced here: 64.7 us
  starting transfers between devices  24.1 us (37%)
  waiting for transfers between devices  18.4 us (28%)
  Pallas kernels  16.1 us (25%)
  local copies, waits for them, and re-layouts  5.91 us (9%)
    ppermute x6, starting transfers between devices, around(): return lax.ppermute(x, 'lon', [(i, (i + d) % n) for i in range(n)])  16.5 us
    pallas_call x1, Pallas kernels, on_device(): pl.pallas_call(functools.partial(row_kernel, n, rows), out_shape=[piece]...  11.4 us
    ppermute x6, waiting for transfers between devices, around(): return lax.ppermute(x, 'lon', [(i, (i + d) % n) for i in range(n)])  10.3 us
    ppermute x4, waiting for transfers between devices, on_device(): edges.append(lax.ppermute(sent[n + k], ('lat', 'lon'), pairs))  8.09 us
    ppermute x4, starting transfers between devices, on_device(): edges.append(lax.ppermute(sent[n + k], ('lat', 'lon'), pairs))  7.68 us
    unnamed x20, local copies, waits for them, and re-layouts  5.69 us
    pallas_call x1, Pallas kernels, on_device(): pl.pallas_call(functools.partial(store_kernel, n, rows), out_shape=jax.Sh...  2.71 us
    pallas_call x1, Pallas kernels, on_device(): pl.pallas_call(functools.partial(send_kernel, n, rows), out_shape=[slab]...  1.96 us
  transfers between devices with their start and end apart: 10, of which 4 were waited for; matrix products, arithmetic and copies ran while one was open for 4% of the time, Pallas kernels for 0%

profile of v1, /device:TPU:12, one launch (start us, length us, event | category | flops | bytes accessed | tf_op | source)
XLA Modules:
  0.0 64.7 jit_solution(14704554218693709003)
XLA Ops:
  0.0 0.9 %copy.23.rotation = s32[8,4]{1,0:T(8,128)S(1)} copy(s32[8,4]{0,1:T(4,128)} %param.21) | data formatting | bytes 256 | tf_op args[9]
  0.9 1.0 %copy-done.2 = bf16[32,32,256]{2,1,0:T(8,128)(2,1)S(1)} copy-done((bf16[32,32,256]{2,1,0:T(8,128)(2,1)S(1)}, bf16[32,32,256]{2,1,0:T(8,128)(2,1)}, u32[]{:S(2)}) %copy-start.2) | copy-done | bytes 524312
  1.9 2.0 %send.1 = (bf16[12,32,256]{2,1,0:T(8,128)(2,1)S(1)}, bf16[12,32,256]{2,1,0:T(8,128)(2,1)S(1)}, bf16[12,32,256]{2,1,0:T(8,128)(2,1)S(1)}, bf16[12,32,256]{2,1,0:T...) custom-call(s32[8,4]{1,0:T(8,128)S(1)} %copy.23.rotation, ...), custom_call_target="tpu_custom_call" | custom-call | tf_op jit(solution)/shard_map/send/pallas_call | solution.py:219
  3.9 1.6 %collective-permute-start = (bf16[12,32,256]{2,1,0:T(8,128)(2,1)S(1)}, bf16[12,32,256]{2,1,0:T(8,128)(2,1)S(1)}, u32[]{:S(2)}, u32[]{:S(2)}) collective-permute-start(bf16[12,32,256]{2,1,0:T(8,128)(2,1)S(1)} %get-tuple-element.18), channel_id=1, source_target_pairs={{0,1},{1,2},{2,3},{3,0},{4,5},{5,6},{6,7},{7,4},{8,9},{9,10},{10,1... | collective-permute-start | bytes 589832 | tf_op jit(solution)/shard_map/ppermute | solution.py:230
  5.5 0.6 collective-permute-start.1
  6.2 1.8 %collective-permute-start.2 = (bf16[12,32,256]{2,1,0:T(8,128)(2,1)S(1)}, bf16[12,32,256]{2,1,0:T(8,128)(2,1)S(1)}, u32[]{:S(2)}, u32[]{:S(2)}) collective-permute-start(bf16[12,32,256]{2,1,0:T(8,128)(2,1)S(1)} %get-tuple-element.20), channel_id=1, source_target_pairs={{0,3},{1,0},{2,1},{3,2},{4,7},{5,4},{6,5},{7,6},{8,11},{9,8},{10,9... | collective-permute-start | bytes 589832 | tf_op jit(solution)/shard_map/ppermute | solution.py:230
  8.0 1.5 %collective-permute-start.3 = (bf16[2,32,256]{2,1,0:T(8,128)(2,1)S(1)}, bf16[2,32,256]{2,1,0:T(8,128)(2,1)S(1)}, u32[]{:S(2)}, u32[]{:S(2)}) collective-permute-start(bf16[2,32,256]{2,1,0:T(8,128)(2,1)S(1)} %get-tuple-element.21), channel_id=1, source_target_pairs={{0,4},{4,8},{8,12},{12,16},{16,20},{20,24},{24,28},{5,3},{9,7},{13... | collective-permute-start | bytes 98312 | tf_op jit(solution)/shard_map/ppermute | solution.py:237
  9.5 4.8 %collective-permute-start.4 = (bf16[2,32,256]{2,1,0:T(8,128)(2,1)S(1)}, bf16[2,32,256]{2,1,0:T(8,128)(2,1)S(1)}, u32[]{:S(2)}, u32[]{:S(2)}) collective-permute-start(bf16[2,32,256]{2,1,0:T(8,128)(2,1)S(1)} %get-tuple-element.22), channel_id=1, source_target_pairs={{1,4},{5,8},{9,12},{13,16},{17,20},{21,24},{25,28},{6,3},{10,7},{1... | collective-permute-start | bytes 98312 | tf_op jit(solution)/shard_map/ppermute | solution.py:237
  14.3 8.1 %collective-permute-done.3.rest_4_ = bf16[2,32,256]{2,1,0:T(8,128)(2,1)S(1)} collective-permute-done((bf16[2,32,256]{2,1,0:T(8,128)(2,1)S(1)}, bf16[2,32,256]{2,1,0:T(8,128)(2,1)S(1)}, u32[]{:S(2)}, u32[]{:S(2)}) %collective-permute-start.3) | collective-permute-done | bytes 32800 | tf_op jit(solution)/shard_map/ppermute | solution.py:237
  22.4 0.7 %collective-permute-start.5 = (bf16[2,32,256]{2,1,0:T(8,128)(2,1)S(1)}, bf16[2,32,256]{2,1,0:T(8,128)(2,1)S(1)}, u32[]{:S(2)}, u32[]{:S(2)}) collective-permute-start(bf16[2,32,256]{2,1,0:T(8,128)(2,1)S(1)} %get-tuple-element.23), channel_id=1, source_target_pairs={{2,4},{6,8},{10,12},{14,16},{18,20},{22,24},{26,28},{7,3},{11,7},{... | collective-permute-start | bytes 98312 | tf_op jit(solution)/shard_map/ppermute | solution.py:237
  23.1 0.7 %collective-permute-start.6 = (bf16[2,32,256]{2,1,0:T(8,128)(2,1)S(1)}, bf16[2,32,256]{2,1,0:T(8,128)(2,1)S(1)}, u32[]{:S(2)}, u32[]{:S(2)}) collective-permute-start(bf16[2,32,256]{2,1,0:T(8,128)(2,1)S(1)} %get-tuple-element.24), channel_id=1, source_target_pairs={{3,4},{7,8},{11,12},{15,16},{19,20},{23,24},{27,28},{4,3},{8,7},{1... | collective-permute-start | bytes 98312 | tf_op jit(solution)/shard_map/ppermute | solution.py:237
  23.8 0.8 %copy.22.owner = s32[8,4]{1,0:T(8,128)S(1)} copy(s32[8,4]{0,1:T(4,128)} %param.22) | data formatting | bytes 256 | tf_op args[10]
  24.5 0.9 %copy.14 = bf16[256,64]{1,0:T(8,128)(2,1)S(1)} copy(bf16[256,64]{0,1:T(8,128)(2,1)} %param.18) | data formatting | bytes 65536 | tf_op args[6]
  25.4 0.9 %copy.18 = bf16[256,64]{1,0:T(8,128)(2,1)S(1)} copy(bf16[256,64]{0,1:T(8,128)(2,1)} %param.19) | data formatting | bytes 65536 | tf_op args[7]
  26.3 0.2 concatenate.3.rest_13_
  26.6 1.3 %copy-done.1 = bf16[3,3,256,256]{3,2,1,0:T(8,128)(2,1)S(1)} copy-done((bf16[3,3,256,256]{3,2,1,0:T(8,128)(2,1)S(1)}, bf16[3,3,256,256]{3,2,1,0:T(8,128)(2,1)}, u32[]{:S(2)}) %copy-start.1) | copy-done | bytes 1179672
  27.9 11.4 %rows.1 = (bf16[8,32,256]{2,1,0:T(8,128)(2,1)S(1)}, bf16[8,32,256]{2,1,0:T(8,128)(2,1)S(1)}, bf16[8,32,256]{2,1,0:T(8,128)(2,1)S(1)}, bf16[8,32,256]{2,1,0:T(8,128)(2,1)S(1)}) custom-call(s32[8,4]{1,0:T(8,128)S(1)} %copy.22.owner, s32[256]{0:T(256)S(1)} %copy-done.5, bf16[12,32,256]{2,1,0:T(8,128)(2,1)S(1)} %get-tuple-element.17.rest_0_, ...), custom_call_target="tpu_custom_call" | custom-call | tf_op jit(solution)/shard_map/rows/pallas_call | solution.py:240
  39.3 0.1 collective-permute-start.7
  39.4 11.0 %collective-permute-start.8 = (bf16[8,32,256]{2,1,0:T(8,128)(2,1)S(1)}, bf16[8,32,256]{2,1,0:T(8,128)(2,1)S(1)}, u32[]{:S(2)}, u32[]{:S(2)}) collective-permute-start(bf16[8,32,256]{2,1,0:T(8,128)(2,1)S(1)} %get-tuple-element.27), channel_id=1, source_target_pairs={{0,2},{1,3},{2,0},{3,1},{4,6},{5,7},{6,4},{7,5},{8,10},{9,11},{10,... | collective-permute-start | bytes 393224 | tf_op jit(solution)/shard_map/ppermute | solution.py:230
  50.3 1.4 %collective-permute-start.9 = (bf16[8,32,256]{2,1,0:T(8,128)(2,1)S(1)}, bf16[8,32,256]{2,1,0:T(8,128)(2,1)S(1)}, u32[]{:S(2)}, u32[]{:S(2)}) collective-permute-start(bf16[8,32,256]{2,1,0:T(8,128)(2,1)S(1)} %get-tuple-element.28), channel_id=1, source_target_pairs={{0,3},{1,0},{2,1},{3,2},{4,7},{5,4},{6,5},{7,6},{8,11},{9,8},{10,9... | collective-permute-start | bytes 393224 | tf_op jit(solution)/shard_map/ppermute | solution.py:230
  51.7 0.6 collective-permute-done.7.rest_1_
  52.3 6.9 %collective-permute-done.8.rest_2_ = bf16[8,32,256]{2,1,0:T(8,128)(2,1)S(1)} collective-permute-done((bf16[8,32,256]{2,1,0:T(8,128)(2,1)S(1)}, bf16[8,32,256]{2,1,0:T(8,128)(2,1)S(1)}, u32[]{:S(2)}, u32[]{:S(2)}) %collective-permute-start.8) | collective-permute-done | bytes 131104 | tf_op jit(solution)/shard_map/ppermute | solution.py:230
  59.2 2.8 %collective-permute-done.9.rest_3_ = bf16[8,32,256]{2,1,0:T(8,128)(2,1)S(1)} collective-permute-done((bf16[8,32,256]{2,1,0:T(8,128)(2,1)S(1)}, bf16[8,32,256]{2,1,0:T(8,128)(2,1)S(1)}, u32[]{:S(2)}, u32[]{:S(2)}) %collective-permute-start.9) | collective-permute-done | bytes 131104 | tf_op jit(solution)/shard_map/ppermute | solution.py:230
  62.0 2.7 %store.1 = bf16[32,32,256]{2,1,0:T(8,128)(2,1)} custom-call(s32[8,4]{1,0:T(8,128)S(1)} %copy.23.rotation, bf16[8,32,256]{2,1,0:T(8,128)(2,1)S(1)} %get-tuple-element.25.rest_0_, bf16[8,32,256]{2,1,0:T(8,128)(2,1)S(1)} %collective-permute-done.7.rest_1_, bf16[8,32,256]{2,1,0:T(8,128)(2,1)S(1)} %collective-permute-done.8.rest_2_, ...), custom_call_target="tpu_custom_call" | custom-call | tf_op jit(solution)/shard_map/store/pallas_call | solution.py:265
  (20 shorter events, 0.0 us)
Async XLA Ops:
  0.0 26.6 %copy-start = (bf16[3,3,256,256]{3,2,1,0:T(8,128)(2,1)S(1)}, bf16[3,3,256,256]{3,2,1,0:T(8,128)(2,1)}, u32[]{:S(2)}) copy-start(bf16[3,3,256,256]{3,2,1,0:T(8,128)(2,1)} %param.13) | copy-start | bytes 3538948
  0.9 1.0 %copy-start.2 = (bf16[32,32,256]{2,1,0:T(8,128)(2,1)S(1)}, bf16[32,32,256]{2,1,0:T(8,128)(2,1)}, u32[]{:S(2)}) copy-start(bf16[32,32,256]{2,1,0:T(8,128)(2,1)} %fields.1) | copy-start | bytes 1572868
  1.9 24.7 %copy-start.3 = (bf16[256,256]{1,0:T(8,128)(2,1)S(1)}, bf16[256,256]{1,0:T(8,128)(2,1)}, u32[]{:S(2)}) copy-start(bf16[256,256]{1,0:T(8,128)(2,1)} %rest_12_.1) | copy-start | bytes 393220
  1.9 24.7 %copy-start.4 = (bf16[256,256]{1,0:T(8,128)(2,1)S(1)}, bf16[256,256]{1,0:T(8,128)(2,1)}, u32[]{:S(2)}) copy-start(bf16[256,256]{1,0:T(8,128)(2,1)} %rest_14_.1) | copy-start | bytes 393220
  1.9 24.7 %copy-start.5 = (s32[256]{0:T(256)S(1)}, s32[256]{0:T(256)}, u32[]{:S(2)}) copy-start(s32[256]{0:T(256)} %counts.1) | copy-start | bytes 3076
  1.9 24.7 %copy-start.6 = (f32[256]{0:T(256)S(1)}, f32[256]{0:T(256)}, u32[]{:S(2)}) copy-start(f32[256]{0:T(256)} %param.14) | copy-start | bytes 3076
  1.9 24.7 %copy-start.7 = (f32[256]{0:T(256)S(1)}, f32[256]{0:T(256)}, u32[]{:S(2)}) copy-start(f32[256]{0:T(256)} %param.16) | copy-start | bytes 3076
  3.9 22.6 %collective-permute-start = (bf16[12,32,256]{2,1,0:T(8,128)(2,1)S(1)}, bf16[12,32,256]{2,1,0:T(8,128)(2,1)S(1)}, u32[]{:S(2)}, u32[]{:S(2)}) collective-permute-start(bf16[12,32,256]{2,1,0:T(8,128)(2,1)S(1)} %get-tuple-element.18), channel_id=1, source_target_pairs={{0,1},{1,2},{2,3},{3,0},{4,5},{5,6},{6,7},{7,4},{8,9},{9,10},{10,1... | collective-permute-start | bytes 589832 | tf_op jit(solution)/shard_map/ppermute | solution.py:230
  5.5 21.0 %collective-permute-start.1 = (bf16[12,32,256]{2,1,0:T(8,128)(2,1)S(1)}, bf16[12,32,256]{2,1,0:T(8,128)(2,1)S(1)}, u32[]{:S(2)}, u32[]{:S(2)}) collective-permute-start(bf16[12,32,256]{2,1,0:T(8,128)(2,1)S(1)} %get-tuple-element.19), channel_id=1, source_target_pairs={{0,2},{1,3},{2,0},{3,1},{4,6},{5,7},{6,4},{7,5},{8,10},{9,11},{10,... | collective-permute-start | bytes 589832 | tf_op jit(solution)/shard_map/ppermute | solution.py:230
  6.2 20.4 %collective-permute-start.2 = (bf16[12,32,256]{2,1,0:T(8,128)(2,1)S(1)}, bf16[12,32,256]{2,1,0:T(8,128)(2,1)S(1)}, u32[]{:S(2)}, u32[]{:S(2)}) collective-permute-start(bf16[12,32,256]{2,1,0:T(8,128)(2,1)S(1)} %get-tuple-element.20), channel_id=1, source_target_pairs={{0,3},{1,0},{2,1},{3,2},{4,7},{5,4},{6,5},{7,6},{8,11},{9,8},{10,9... | collective-permute-start | bytes 589832 | tf_op jit(solution)/shard_map/ppermute | solution.py:230
  8.0 14.5 %collective-permute-start.3 = (bf16[2,32,256]{2,1,0:T(8,128)(2,1)S(1)}, bf16[2,32,256]{2,1,0:T(8,128)(2,1)S(1)}, u32[]{:S(2)}, u32[]{:S(2)}) collective-permute-start(bf16[2,32,256]{2,1,0:T(8,128)(2,1)S(1)} %get-tuple-element.21), channel_id=1, source_target_pairs={{0,4},{4,8},{8,12},{12,16},{16,20},{20,24},{24,28},{5,3},{9,7},{13... | collective-permute-start | bytes 98312 | tf_op jit(solution)/shard_map/ppermute | solution.py:237
  9.5 13.6 %collective-permute-start.4 = (bf16[2,32,256]{2,1,0:T(8,128)(2,1)S(1)}, bf16[2,32,256]{2,1,0:T(8,128)(2,1)S(1)}, u32[]{:S(2)}, u32[]{:S(2)}) collective-permute-start(bf16[2,32,256]{2,1,0:T(8,128)(2,1)S(1)} %get-tuple-element.22), channel_id=1, source_target_pairs={{1,4},{5,8},{9,12},{13,16},{17,20},{21,24},{25,28},{6,3},{10,7},{1... | collective-permute-start | bytes 98312 | tf_op jit(solution)/shard_map/ppermute | solution.py:237
  22.4 4.1 %collective-permute-start.5 = (bf16[2,32,256]{2,1,0:T(8,128)(2,1)S(1)}, bf16[2,32,256]{2,1,0:T(8,128)(2,1)S(1)}, u32[]{:S(2)}, u32[]{:S(2)}) collective-permute-start(bf16[2,32,256]{2,1,0:T(8,128)(2,1)S(1)} %get-tuple-element.23), channel_id=1, source_target_pairs={{2,4},{6,8},{10,12},{14,16},{18,20},{22,24},{26,28},{7,3},{11,7},{... | collective-permute-start | bytes 98312 | tf_op jit(solution)/shard_map/ppermute | solution.py:237
  23.1 3.4 %collective-permute-start.6 = (bf16[2,32,256]{2,1,0:T(8,128)(2,1)S(1)}, bf16[2,32,256]{2,1,0:T(8,128)(2,1)S(1)}, u32[]{:S(2)}, u32[]{:S(2)}) collective-permute-start(bf16[2,32,256]{2,1,0:T(8,128)(2,1)S(1)} %get-tuple-element.24), channel_id=1, source_target_pairs={{3,4},{7,8},{11,12},{15,16},{19,20},{23,24},{27,28},{4,3},{8,7},{1... | collective-permute-start | bytes 98312 | tf_op jit(solution)/shard_map/ppermute | solution.py:237
  26.6 1.3 %copy-start.1 = (bf16[3,3,256,256]{3,2,1,0:T(8,128)(2,1)S(1)}, bf16[3,3,256,256]{3,2,1,0:T(8,128)(2,1)}, u32[]{:S(2)}) copy-start(bf16[3,3,256,256]{3,2,1,0:T(8,128)(2,1)} %param.15) | copy-start | bytes 3538948
  39.3 13.0 %collective-permute-start.7 = (bf16[8,32,256]{2,1,0:T(8,128)(2,1)S(1)}, bf16[8,32,256]{2,1,0:T(8,128)(2,1)S(1)}, u32[]{:S(2)}, u32[]{:S(2)}) collective-permute-start(bf16[8,32,256]{2,1,0:T(8,128)(2,1)S(1)} %get-tuple-element.26), channel_id=1, source_target_pairs={{0,1},{1,2},{2,3},{3,0},{4,5},{5,6},{6,7},{7,4},{8,9},{9,10},{10,1... | collective-permute-start | bytes 393224 | tf_op jit(solution)/shard_map/ppermute | solution.py:230
  39.4 19.9 %collective-permute-start.8 = (bf16[8,32,256]{2,1,0:T(8,128)(2,1)S(1)}, bf16[8,32,256]{2,1,0:T(8,128)(2,1)S(1)}, u32[]{:S(2)}, u32[]{:S(2)}) collective-permute-start(bf16[8,32,256]{2,1,0:T(8,128)(2,1)S(1)} %get-tuple-element.27), channel_id=1, source_target_pairs={{0,2},{1,3},{2,0},{3,1},{4,6},{5,7},{6,4},{7,5},{8,10},{9,11},{10,... | collective-permute-start | bytes 393224 | tf_op jit(solution)/shard_map/ppermute | solution.py:230
  50.3 11.7 %collective-permute-start.9 = (bf16[8,32,256]{2,1,0:T(8,128)(2,1)S(1)}, bf16[8,32,256]{2,1,0:T(8,128)(2,1)S(1)}, u32[]{:S(2)}, u32[]{:S(2)}) collective-permute-start(bf16[8,32,256]{2,1,0:T(8,128)(2,1)S(1)} %get-tuple-element.28), channel_id=1, source_target_pairs={{0,3},{1,0},{2,1},{3,2},{4,7},{5,4},{6,5},{7,6},{8,11},{9,8},{10,9... | collective-permute-start | bytes 393224 | tf_op jit(solution)/shard_map/ppermute | solution.py:230

commit v2 on v1

v2 whole, which is shorter than its diff:
```python
import functools

import jax
import jax.numpy as jnp
from jax import lax
from jax.experimental import pallas as pl
from jax.experimental.pallas import tpu as pltpu
from jax.sharding import PartitionSpec as P

HALO = 2
LANES = 128
GROUP = 256
VMEM_BYTES = 28 * 1024 * 1024


def group_of(band, shard, n):
    return jnp.where(band % 2 == 0, shard, n - 1 - shard)


def shard_of(band, group, n):
    return group if band % 2 == 0 else n - 1 - group


def first_held(group, rows):
    return group * rows - HALO * (group % 2)


def turn(quarter, staged, block, out):
    size, _, chans = out.shape
    tiles = staged.shape[0]

    def column(col):
        parts = [staged[t, pl.ds(col, size, stride=size), :] for t in range(tiles)]
        return jnp.concatenate(parts, axis=1).astype(jnp.bfloat16)

    def keep(i, row):
        for t in range(tiles):
            staged[t, pl.ds(i * size, size), :] = row[:, t * LANES : (t + 1) * LANES]

    @pl.when(quarter == 0)
    def _():
        out[...] = block[...]

    @pl.when(quarter == 1)
    def _():
        for i in range(size):
            keep(i, block[i].astype(jnp.float32))
        for i in range(size):
            out[i] = column(size - 1 - i)

    @pl.when(quarter == 2)
    def _():
        depth = GROUP // size
        i = lax.broadcasted_iota(jnp.int32, (GROUP, GROUP), 0)
        j = lax.broadcasted_iota(jnp.int32, (GROUP, GROUP), 1)
        backwards = jnp.where(i + j == GROUP - 1, 1.0, 0.0).astype(jnp.bfloat16)
        for g in range(size // depth):
            cells = block[size - (g + 1) * depth : size - g * depth].reshape(GROUP, chans)
            turned = jnp.dot(backwards, cells, preferred_element_type=jnp.float32).astype(jnp.bfloat16)
            out[g * depth : (g + 1) * depth] = turned.reshape(depth, size, chans)

    @pl.when(quarter == 3)
    def _():
        for i in range(size):
            keep(size - 1 - i, block[i].astype(jnp.float32))
        for i in range(size):
            out[i] = column(i)


def send_kernel(n, rows, rotation, fields, *rest):
    slabs = rest[:n]
    staged, upright = rest[n:]
    band = lax.axis_index("lat")
    me = lax.axis_index("lon")
    turn((4 - rotation[me, band]) % 4, staged, fields, upright)
    for d in range(n):
        group = group_of(band, lax.rem(me + d, n), n)
        slabs[d][...] = upright[pl.ds(first_held(group, rows), rows + HALO)]


def columns_of(segment, size):
    return pl.ds(pl.multiple_of(segment * size, size), size)


def gather_kernel(n, rows, owner, *rest):
    slabs = rest[:n]
    grid, edge = rest[n:]
    band = lax.axis_index("lat")
    me = lax.axis_index("lon")
    group = group_of(band, me, n)
    size = slabs[0].shape[1]
    for d in range(n):
        source = lax.rem(me + n - d, n)
        grid[:, columns_of(owner[source, band], size)] = slabs[d][...]
    edge[...] = grid[pl.ds(rows * (group % 2), HALO)]


def spread(taps, r, row):
    cols, chans = row.shape
    taps[r, :, :chans] = pltpu.roll(row, 1, 0).astype(jnp.bfloat16)
    taps[r, :, chans : 2 * chans] = row.astype(jnp.bfloat16)
    taps[r, :, 2 * chans :] = pltpu.roll(row, cols - 1, 0).astype(jnp.bfloat16)


def convolve(taps, weight, bias, count):
    cols, width = taps.shape[1:]
    total = bias[...]
    for i in range(3):
        window = taps[i : i + count].reshape(count * cols, width)
        total = total + jnp.dot(window, weight[i], preferred_element_type=jnp.float32)
    return total


def silu(x):
    return x / (1.0 + jnp.exp(-x))


def live_count(counts, row):
    inside = (row >= 0) & (row < counts.shape[0])
    return jnp.where(inside, counts[jnp.clip(row, 0, counts.shape[0] - 1)], 0)


def first_kernel(n, rows, size, counts, grid, weight, bias, acts, taps):
    band = lax.axis_index("lat")
    group = group_of(band, lax.axis_index("lon"), n)
    cols, chans = grid.shape[1:]
    cell = lax.broadcasted_iota(jnp.int32, (cols, chans), 0)
    top = band * size + first_held(group, rows) + 1
    for r in range(rows + HALO):
        spread(taps, r, grid[r].astype(jnp.float32))
    act = silu(convolve(taps, weight, bias, rows))
    for r in range(rows):
        live = cell < live_count(counts, top + r)
        spread(acts, r, jnp.where(live, act[r * cols : (r + 1) * cols], 0.0))


def rows_kernel(n, rows, size, owner, counts, *rest):
    grid, acts, sent, received = rest[:4]
    w_conv1, b_conv1, w_conv2, b_conv2, w_qv, w_key, w_out = rest[4:11]
    results = rest[11 : n + 11]
    taps1, taps2, mixed, attended = rest[n + 11 :]
    band = lax.axis_index("lat")
    me = lax.axis_index("lon")
    group = group_of(band, me, n)
    odd = group % 2
    cols, chans = grid.shape[1:]
    head_dim = w_key.shape[0]
    heads = chans // head_dim
    cell = lax.broadcasted_iota(jnp.int32, (cols, chans), 0)
    first_row = band * size + group * rows

    for r in range(HALO):
        spread(taps1, r + HALO * (1 - odd), sent[r].astype(jnp.float32))
        spread(taps1, r + HALO * odd, received[r].astype(jnp.float32))
    taps2[pl.ds(HALO * (1 - odd), rows)] = acts[...]
    act = silu(convolve(taps1, w_conv1, b_conv1, HALO))
    for r in range(HALO):
        at = r + rows * odd
        live = cell < live_count(counts, first_row + at - 1)
        spread(taps2, at, jnp.where(live, act[r * cols : (r + 1) * cols], 0.0))
    second = convolve(taps2, w_conv2, b_conv2, rows)

    for r in range(rows):
        live = cell < counts[first_row + r]
        here = grid[r + HALO * odd].astype(jnp.float32)
        part = jnp.where(live, here + second[r * cols : (r + 1) * cols], 0.0)
        mixed[r * cols : (r + 1) * cols, :] = part.astype(jnp.bfloat16)
    flat = mixed[...].astype(jnp.float32)
    normed = (flat * lax.rsqrt(jnp.mean(flat * flat, axis=1, keepdims=True) + 1e-06)).astype(jnp.bfloat16)

    def by_last(a, b):
        return lax.dot_general(a, b, (((1,), (1,)), ((), ())), preferred_element_type=jnp.float32)

    keys = by_last(normed, w_key[...]).astype(jnp.bfloat16)
    flipped = by_last(w_qv[...], normed).astype(jnp.bfloat16)
    key_at = lax.broadcasted_iota(jnp.int32, (cols, heads * cols), 0)
    scale = 1.0 / head_dim**0.5
    for r in range(rows):
        at = slice(r * cols, (r + 1) * cols)
        queries = jnp.concatenate([flipped[h * head_dim : (h + 1) * head_dim, at] for h in range(heads)], axis=1)
        scores = jnp.dot(keys[at], queries, preferred_element_type=jnp.float32)
        scores = jnp.where(key_at < counts[first_row + r], scores * scale, -jnp.inf)
        expo = jnp.exp(scores - jnp.max(scores, axis=0, keepdims=True))
        total = jnp.sum(expo, axis=0, keepdims=True)
        summed = jnp.dot(flipped[chans:, at], expo.astype(jnp.bfloat16), preferred_element_type=jnp.float32)
        share = (summed / total).astype(jnp.bfloat16)
        for h in range(heads):
            attended[h * head_dim : (h + 1) * head_dim, at] = share[:, h * cols : (h + 1) * cols]
    update = lax.dot_general(attended[...], w_out[...], (((0,), (0,)), ((), ())), preferred_element_type=jnp.float32)
    for r in range(rows):
        at = slice(r * cols, (r + 1) * cols)
        live = cell < counts[first_row + r]
        mixed[at, :] = (mixed[at, :].astype(jnp.float32) + jnp.where(live, update[at], 0.0)).astype(jnp.bfloat16)
    for d in range(n):
        segment = owner[lax.rem(me + d, n), band]
        for r in range(rows):
            results[d][r] = mixed[columns_of(segment + r * n, size), :]


def store_kernel(n, rows, rotation, *rest):
    slabs = rest[:n]
    out, staged, upright = rest[n:]
    band = lax.axis_index("lat")
    me = lax.axis_index("lon")
    for d in range(n):
        group = group_of(band, lax.rem(me + n - d, n), n)
        upright[pl.ds(group * rows, rows)] = slabs[d][...]
    turn(rotation[me, band] % 4, staged, upright, out)


def on_device(
    bands,
    n,
    fields,
    w_conv1,
    b_conv1,
    w_conv2,
    b_conv2,
    w_query,
    w_key,
    w_value,
    w_out,
    rotation,
    owner,
    counts,
):
    size, _, chans = fields.shape
    rows = size // n
    cols = size * n
    bf16 = jnp.bfloat16
    smem = pl.BlockSpec(memory_space=pltpu.SMEM)
    vmem = pl.BlockSpec(memory_space=pltpu.VMEM)
    params = pltpu.CompilerParams(vmem_limit_bytes=VMEM_BYTES)
    staging = pltpu.VMEM((chans // LANES, size * size, LANES), jnp.float32)
    block = pltpu.VMEM((size, size, chans), bf16)

    def call(kernel, name, out, scalars, arrays, scratch):
        many = isinstance(out, list)
        return pl.pallas_call(
            functools.partial(kernel, n, rows),
            out_shape=out,
            in_specs=[smem] * len(scalars) + [vmem] * len(arrays),
            out_specs=[vmem] * len(out) if many else vmem,
            scratch_shapes=scratch,
            compiler_params=params,
            name=name,
        )(*scalars, *arrays)

    def array(*shape):
        return jax.ShapeDtypeStruct(shape, bf16)

    def around(parts):
        pairs = [[(i, (i + d) % n) for i in range(n)] for d in range(n)]
        return [parts[0]] + [lax.ppermute(parts[d], "lon", pairs[d]) for d in range(1, n)]

    rotation, owner = rotation.T, owner.T
    w_first = w_conv1.reshape(3, 3 * chans, chans)
    w_second = w_conv2.reshape(3, 3 * chans, chans)
    b_first = b_conv1.reshape(1, chans)
    b_second = b_conv2.reshape(1, chans)
    w_qv = jnp.concatenate([w_query.T, w_value.T], axis=0)

    slabs = [array(rows + HALO, size, chans)] * n
    slabs = around(call(send_kernel, "send", slabs, [rotation], [fields], [staging, block]))
    held = [array(rows + HALO, cols, chans), array(HALO, cols, chans)]
    grid, sent = call(gather_kernel, "gather", held, [owner], slabs, [])
    snake = [a * n + shard_of(a, g, n) for a in range(bands) for g in range(n)]
    pairs = [(snake[i], snake[i + 1 if i % 2 else i - 1]) for i in range(1, bands * n - 1)]
    received = lax.ppermute(sent, ("lat", "lon"), pairs)
    acts = call(
        lambda n, rows, *refs: first_kernel(n, rows, size, *refs),
        "first",
        array(rows, cols, 3 * chans),
        [counts],
        [grid, w_first, b_first],
        [pltpu.VMEM((rows + HALO, cols, 3 * chans), bf16)],
    )
    results = call(
        lambda n, rows, *refs: rows_kernel(n, rows, size, *refs),
        "rows",
        [array(rows, size, chans)] * n,
        [owner, counts],
        [grid, acts, sent, received, w_first, b_first, w_second, b_second, w_qv, w_key.T, w_out],
        [
            pltpu.VMEM((2 * HALO, cols, 3 * chans), bf16),
            pltpu.VMEM((rows + HALO, cols, 3 * chans), bf16),
            pltpu.VMEM((rows * cols, chans), bf16),
            pltpu.VMEM((chans, rows * cols), bf16),
        ],
    )
    results = around(results)
    return call(store_kernel, "store", array(*fields.shape), [rotation], results, [staging, block])


def solution(mesh):
    in_specs = (P("lat", "lon", None), P(), P(), P(), P(), P(), P(), P(), P(), P(), P(), P())
    out_specs = P("lat", "lon", None)
    body = functools.partial(on_device, mesh.shape["lat"], mesh.shape["lon"])
    return jax.shard_map(body, mesh=mesh, in_specs=in_specs, out_specs=out_specs, check_vma=False)
```

time: 65 us -> 51.8 us (0.80)
  the two profiles are of different devices: /device:TPU:12 before, /device:TPU:11 now
where the time goes in v2:
time: 51.8 us; the launch traced here: 51.7 us
  waiting for transfers between devices  25.3 us (49%)
  Pallas kernels  13.2 us (25%)
  starting transfers between devices  8.7 us (17%)
  local copies, waits for them, and re-layouts  3.55 us (7%)
  other arithmetic  0.77 us (1%)
    ppermute x6, waiting for transfers between devices, around(): lax.ppermute(parts[d], 'lon', pairs[d])  24.8 us
    pallas_call x5, Pallas kernels, call(): pl.pallas_call(functools.partial(kernel, n, rows), out_shape=out, in_spec...  13.2 us
    ppermute x6, starting transfers between devices, around(): lax.ppermute(parts[d], 'lon', pairs[d])  6.78 us
    unnamed x25, local copies, waits for them, and re-layouts  3.55 us
    ppermute x1, starting transfers between devices, on_device(): received = lax.ppermute(sent, ('lat', 'lon'), pairs)  1.92 us
  transfers between devices with their start and end apart: 7, of which 7 were waited for; matrix products, arithmetic and copies ran while one was open for 3% of the time, Pallas kernels for 4%

profile of v2, /device:TPU:11, one launch (start us, length us, event | category | flops | bytes accessed | tf_op | source)
XLA Modules:
  0.0 51.7 jit_solution(10101140687752279560)
XLA Ops:
  0.0 1.1 %copy-done.2 = bf16[32,32,256]{2,1,0:T(8,128)(2,1)S(1)} copy-done((bf16[32,32,256]{2,1,0:T(8,128)(2,1)S(1)}, bf16[32,32,256]{2,1,0:T(8,128)(2,1)}, u32[]{:S(2)}) %copy-start.2) | copy-done | bytes 524312
  1.1 0.7 %copy-done.7 = s32[8,4]{0,1:T(4,128)S(1)} copy-done((s32[8,4]{0,1:T(4,128)S(1)}, s32[8,4]{0,1:T(4,128)}, u32[]{:S(2)}) %copy-start.7) | copy-done | bytes 152
  1.8 1.3 %send.1 = (bf16[10,32,256]{2,1,0:T(8,128)(2,1)S(1)}, bf16[10,32,256]{2,1,0:T(8,128)(2,1)S(1)}, bf16[10,32,256]{2,1,0:T(8,128)(2,1)S(1)}, bf16[10,32,256]{2,1,0:T(8,128)(2,1)S(1)}) custom-call(s32[4,8]{1,0:T(4,128)S(1)} %bitcast.15, bf16[32,32,256]{2,1,0:T(8,128)(2,1)S(1)} %copy-done.2), custom_call_target="tpu_custom_call" | custom-call | tf_op jit(solution)/shard_map/send/pallas_call | solution.py:239
  3.1 1.3 %collective-permute-start = (bf16[10,32,256]{2,1,0:T(8,128)(2,1)S(1)}, bf16[10,32,256]{2,1,0:T(8,128)(2,1)S(1)}, u32[]{:S(2)}, u32[]{:S(2)}) collective-permute-start(bf16[10,32,256]{2,1,0:T(8,128)(2,1)S(1)} %get-tuple-element.16), channel_id=1, source_target_pairs={{0,1},{1,2},{2,3},{3,0},{4,5},{5,6},{6,7},{7,4},{8,9},{9,10},{10,1... | collective-permute-start | bytes 491528 | tf_op jit(solution)/shard_map/ppermute | solution.py:254
  4.5 1.1 %collective-permute-start.1 = (bf16[10,32,256]{2,1,0:T(8,128)(2,1)S(1)}, bf16[10,32,256]{2,1,0:T(8,128)(2,1)S(1)}, u32[]{:S(2)}, u32[]{:S(2)}) collective-permute-start(bf16[10,32,256]{2,1,0:T(8,128)(2,1)S(1)} %get-tuple-element.17), channel_id=1, source_target_pairs={{0,2},{1,3},{2,0},{3,1},{4,6},{5,7},{6,4},{7,5},{8,10},{9,11},{10,... | collective-permute-start | bytes 491528 | tf_op jit(solution)/shard_map/ppermute | solution.py:254
  5.6 1.4 %collective-permute-start.2 = (bf16[10,32,256]{2,1,0:T(8,128)(2,1)S(1)}, bf16[10,32,256]{2,1,0:T(8,128)(2,1)S(1)}, u32[]{:S(2)}, u32[]{:S(2)}) collective-permute-start(bf16[10,32,256]{2,1,0:T(8,128)(2,1)S(1)} %get-tuple-element.18), channel_id=1, source_target_pairs={{0,3},{1,0},{2,1},{3,2},{4,7},{5,4},{6,5},{7,6},{8,11},{9,8},{10,9... | collective-permute-start | bytes 491528 | tf_op jit(solution)/shard_map/ppermute | solution.py:254
  7.0 1.7 %collective-permute-done.rest_1_ = bf16[10,32,256]{2,1,0:T(8,128)(2,1)S(1)} collective-permute-done((bf16[10,32,256]{2,1,0:T(8,128)(2,1)S(1)}, bf16[10,32,256]{2,1,0:T(8,128)(2,1)S(1)}, u32[]{:S(2)}, u32[]{:S(2)}) %collective-permute-start) | collective-permute-done | bytes 163872 | tf_op jit(solution)/shard_map/ppermute | solution.py:254
  8.7 9.2 %collective-permute-done.1.rest_2_ = bf16[10,32,256]{2,1,0:T(8,128)(2,1)S(1)} collective-permute-done((bf16[10,32,256]{2,1,0:T(8,128)(2,1)S(1)}, bf16[10,32,256]{2,1,0:T(8,128)(2,1)S(1)}, u32[]{:S(2)}, u32[]{:S(2)}) %collective-permute-start.1) | collective-permute-done | bytes 163872 | tf_op jit(solution)/shard_map/ppermute | solution.py:254
  17.9 2.8 %collective-permute-done.2.rest_3_ = bf16[10,32,256]{2,1,0:T(8,128)(2,1)S(1)} collective-permute-done((bf16[10,32,256]{2,1,0:T(8,128)(2,1)S(1)}, bf16[10,32,256]{2,1,0:T(8,128)(2,1)S(1)}, u32[]{:S(2)}, u32[]{:S(2)}) %collective-permute-start.2) | collective-permute-done | bytes 163872 | tf_op jit(solution)/shard_map/ppermute | solution.py:254
  20.7 0.7 %copy-done.5 = s32[8,4]{0,1:T(4,128)S(1)} copy-done((s32[8,4]{0,1:T(4,128)S(1)}, s32[8,4]{0,1:T(4,128)}, u32[]{:S(2)}) %copy-start.5) | copy-done | bytes 152
  21.4 0.6 %gather.1 = (bf16[10,128,256]{2,1,0:T(8,128)(2,1)S(1)}, bf16[2,128,256]{2,1,0:T(8,128)(2,1)S(1)}) custom-call(s32[4,8]{1,0:T(4,128)S(1)} %bitcast.13, bf16[10,32,256]{2,1,0:T(8,128)(2,1)S(1)} %get-tuple-element.15.rest_0_, bf16[10,32,256]{2,1,0:T(8,128)(2,1)S(1)} %collective-permute-done.rest_1_, bf16[10,32,256]{2,1,0:T(8,128)(2,1)S(1)} %collective-permute-done.1.rest_2_, ...), custom_call_target="tpu_custom_call" | custom-call | tf_op jit(solution)/shard_map/gather/pallas_call | solution.py:239
  22.0 1.9 %collective-permute-start.3 = (bf16[2,128,256]{2,1,0:T(8,128)(2,1)S(1)}, bf16[2,128,256]{2,1,0:T(8,128)(2,1)S(1)}, u32[]{:S(2)}, u32[]{:S(2)}) collective-permute-start(bf16[2,128,256]{2,1,0:T(8,128)(2,1)S(1)} %get-tuple-element.20.refs_4_), channel_id=1, source_target_pairs={{1,2},{2,1},{3,7},{7,3},{6,5},{5,6},{4,8},{8,4},{9,10},{10,9},{11,... | collective-permute-start | bytes 393224 | tf_op jit(solution)/shard_map/ppermute | solution.py:269
  24.0 1.0 %copy.13 = bf16[256,256]{0,1:T(8,128)(2,1)S(1)} copy(bf16[256,256]{1,0:T(8,128)(2,1)} %param.17) | data formatting | bytes 262144 | tf_op args[5]
  25.0 0.8 %pad_maximum_fusion.refs_10_ = bf16[320,256]{1,0:T(8,128)(2,1)S(1)} fusion(bf16[64,256]{1,0:T(8,128)(2,1)} %bitcast.21, bf16[256,256]{1,0:T(8,128)(2,1)S(1)} %bitcast.20), kind=kLoop, calls=%fused_computation | loop fusion | flops 327680 | bytes 327680 | tf_op jit(solution)/shard_map/concatenate | solution.py:261
  25.8 2.2 %first.1.refs_3_ = bf16[8,128,768]{2,1,0:T(8,128)(2,1)S(1)} custom-call(s32[256]{0:T(256)S(1)} %copy-done.9, bf16[10,128,256]{2,1,0:T(8,128)(2,1)S(1)} %get-tuple-element.19.refs_1_.refs_2_, bf16[3,768,256]{2,1,0:T(8,128)(2,1)S(1)} %bitcast.9, f32[1,256]{1,0:T(1,128)S(1)} %bitcast.17), custom_call_target="tpu_custom_call" | custom-call | tf_op jit(solution)/shard_map/first/pallas_call | solution.py:239
  28.1 0.4 collective-permute-done.3.refs_5_
  28.5 7.0 %rows.1 = (bf16[8,32,256]{2,1,0:T(8,128)(2,1)S(1)}, bf16[8,32,256]{2,1,0:T(8,128)(2,1)S(1)}, bf16[8,32,256]{2,1,0:T(8,128)(2,1)S(1)}, bf16[8,32,256]{2,1,0:T(8,128)(2,1)S(1)}) custom-call(s32[4,8]{1,0:T(4,128)S(1)} %bitcast.14, s32[256]{0:T(256)S(1)} %copy-done.9, bf16[10,128,256]{2,1,0:T(8,128)(2,1)S(1)} %get-tuple-element.19.refs_1_.refs_2_, ...), custom_call_target="tpu_custom_call" | custom-call | tf_op jit(solution)/shard_map/rows/pallas_call | solution.py:239
  35.5 1.1 %collective-permute-start.4 = (bf16[8,32,256]{2,1,0:T(8,128)(2,1)S(1)}, bf16[8,32,256]{2,1,0:T(8,128)(2,1)S(1)}, u32[]{:S(2)}, u32[]{:S(2)}) collective-permute-start(bf16[8,32,256]{2,1,0:T(8,128)(2,1)S(1)} %get-tuple-element.22), channel_id=1, source_target_pairs={{0,1},{1,2},{2,3},{3,0},{4,5},{5,6},{6,7},{7,4},{8,9},{9,10},{10,1... | collective-permute-start | bytes 393224 | tf_op jit(solution)/shard_map/ppermute | solution.py:254
  36.6 0.8 %collective-permute-start.5 = (bf16[8,32,256]{2,1,0:T(8,128)(2,1)S(1)}, bf16[8,32,256]{2,1,0:T(8,128)(2,1)S(1)}, u32[]{:S(2)}, u32[]{:S(2)}) collective-permute-start(bf16[8,32,256]{2,1,0:T(8,128)(2,1)S(1)} %get-tuple-element.23), channel_id=1, source_target_pairs={{0,2},{1,3},{2,0},{3,1},{4,6},{5,7},{6,4},{7,5},{8,10},{9,11},{10,... | collective-permute-start | bytes 393224 | tf_op jit(solution)/shard_map/ppermute | solution.py:254
  37.4 1.1 %collective-permute-start.6 = (bf16[8,32,256]{2,1,0:T(8,128)(2,1)S(1)}, bf16[8,32,256]{2,1,0:T(8,128)(2,1)S(1)}, u32[]{:S(2)}, u32[]{:S(2)}) collective-permute-start(bf16[8,32,256]{2,1,0:T(8,128)(2,1)S(1)} %get-tuple-element.24), channel_id=1, source_target_pairs={{0,3},{1,0},{2,1},{3,2},{4,7},{5,4},{6,5},{7,6},{8,11},{9,8},{10,9... | collective-permute-start | bytes 393224 | tf_op jit(solution)/shard_map/ppermute | solution.py:254
  38.5 0.9 %collective-permute-done.4.rest_1_ = bf16[8,32,256]{2,1,0:T(8,128)(2,1)S(1)} collective-permute-done((bf16[8,32,256]{2,1,0:T(8,128)(2,1)S(1)}, bf16[8,32,256]{2,1,0:T(8,128)(2,1)S(1)}, u32[]{:S(2)}, u32[]{:S(2)}) %collective-permute-start.4) | collective-permute-done | bytes 131104 | tf_op jit(solution)/shard_map/ppermute | solution.py:254
  39.4 7.7 %collective-permute-done.5.rest_2_ = bf16[8,32,256]{2,1,0:T(8,128)(2,1)S(1)} collective-permute-done((bf16[8,32,256]{2,1,0:T(8,128)(2,1)S(1)}, bf16[8,32,256]{2,1,0:T(8,128)(2,1)S(1)}, u32[]{:S(2)}, u32[]{:S(2)}) %collective-permute-start.5) | collective-permute-done | bytes 131104 | tf_op jit(solution)/shard_map/ppermute | solution.py:254
  47.1 2.5 %collective-permute-done.6.rest_3_ = bf16[8,32,256]{2,1,0:T(8,128)(2,1)S(1)} collective-permute-done((bf16[8,32,256]{2,1,0:T(8,128)(2,1)S(1)}, bf16[8,32,256]{2,1,0:T(8,128)(2,1)S(1)}, u32[]{:S(2)}, u32[]{:S(2)}) %collective-permute-start.6) | collective-permute-done | bytes 131104 | tf_op jit(solution)/shard_map/ppermute | solution.py:254
  49.6 2.1 %store.1 = bf16[32,32,256]{2,1,0:T(8,128)(2,1)} custom-call(s32[4,8]{1,0:T(4,128)S(1)} %bitcast.16, bf16[8,32,256]{2,1,0:T(8,128)(2,1)S(1)} %get-tuple-element.21.rest_0_, bf16[8,32,256]{2,1,0:T(8,128)(2,1)S(1)} %collective-permute-done.4.rest_1_, bf16[8,32,256]{2,1,0:T(8,128)(2,1)S(1)} %collective-permute-done.5.rest_2_, ...), custom_call_target="tpu_custom_call" | custom-call | tf_op jit(solution)/shard_map/store/pallas_call | solution.py:239
  (21 shorter events, 0.1 us)
Async XLA Ops:
  0.0 25.7 %copy-start = (bf16[3,3,256,256]{3,2,1,0:T(8,128)(2,1)S(1)}, bf16[3,3,256,256]{3,2,1,0:T(8,128)(2,1)}, u32[]{:S(2)}) copy-start(bf16[3,3,256,256]{3,2,1,0:T(8,128)(2,1)} %param.13) | copy-start | bytes 3538948
  0.0 1.1 %copy-start.2 = (bf16[32,32,256]{2,1,0:T(8,128)(2,1)S(1)}, bf16[32,32,256]{2,1,0:T(8,128)(2,1)}, u32[]{:S(2)}) copy-start(bf16[32,32,256]{2,1,0:T(8,128)(2,1)} %fields.1) | copy-start | bytes 1572868
  1.1 0.7 %copy-start.7 = (s32[8,4]{0,1:T(4,128)S(1)}, s32[8,4]{0,1:T(4,128)}, u32[]{:S(2)}) copy-start(s32[8,4]{0,1:T(4,128)} %param.21) | copy-start | bytes 388
  3.1 5.5 %collective-permute-start = (bf16[10,32,256]{2,1,0:T(8,128)(2,1)S(1)}, bf16[10,32,256]{2,1,0:T(8,128)(2,1)S(1)}, u32[]{:S(2)}, u32[]{:S(2)}) collective-permute-start(bf16[10,32,256]{2,1,0:T(8,128)(2,1)S(1)} %get-tuple-element.16), channel_id=1, source_target_pairs={{0,1},{1,2},{2,3},{3,0},{4,5},{5,6},{6,7},{7,4},{8,9},{9,10},{10,1... | collective-permute-start | bytes 491528 | tf_op jit(solution)/shard_map/ppermute | solution.py:254
  4.5 13.4 %collective-permute-start.1 = (bf16[10,32,256]{2,1,0:T(8,128)(2,1)S(1)}, bf16[10,32,256]{2,1,0:T(8,128)(2,1)S(1)}, u32[]{:S(2)}, u32[]{:S(2)}) collective-permute-start(bf16[10,32,256]{2,1,0:T(8,128)(2,1)S(1)} %get-tuple-element.17), channel_id=1, source_target_pairs={{0,2},{1,3},{2,0},{3,1},{4,6},{5,7},{6,4},{7,5},{8,10},{9,11},{10,... | collective-permute-start | bytes 491528 | tf_op jit(solution)/shard_map/ppermute | solution.py:254
  5.6 15.1 %collective-permute-start.2 = (bf16[10,32,256]{2,1,0:T(8,128)(2,1)S(1)}, bf16[10,32,256]{2,1,0:T(8,128)(2,1)S(1)}, u32[]{:S(2)}, u32[]{:S(2)}) collective-permute-start(bf16[10,32,256]{2,1,0:T(8,128)(2,1)S(1)} %get-tuple-element.18), channel_id=1, source_target_pairs={{0,3},{1,0},{2,1},{3,2},{4,7},{5,4},{6,5},{7,6},{8,11},{9,8},{10,9... | collective-permute-start | bytes 491528 | tf_op jit(solution)/shard_map/ppermute | solution.py:254
  20.7 0.7 %copy-start.5 = (s32[8,4]{0,1:T(4,128)S(1)}, s32[8,4]{0,1:T(4,128)}, u32[]{:S(2)}) copy-start(s32[8,4]{0,1:T(4,128)} %param.22) | copy-start | bytes 388
  21.4 4.4 %copy-start.9 = (s32[256]{0:T(256)S(1)}, s32[256]{0:T(256)}, u32[]{:S(2)}) copy-start(s32[256]{0:T(256)} %refs_1_.1) | copy-start | bytes 3076
  21.4 4.4 %copy-start.10 = (f32[256]{0:T(256)S(1)}, f32[256]{0:T(256)}, u32[]{:S(2)}) copy-start(f32[256]{0:T(256)} %param.14) | copy-start | bytes 3076
  22.0 6.5 %collective-permute-start.3 = (bf16[2,128,256]{2,1,0:T(8,128)(2,1)S(1)}, bf16[2,128,256]{2,1,0:T(8,128)(2,1)S(1)}, u32[]{:S(2)}, u32[]{:S(2)}) collective-permute-start(bf16[2,128,256]{2,1,0:T(8,128)(2,1)S(1)} %get-tuple-element.20.refs_4_), channel_id=1, source_target_pairs={{1,2},{2,1},{3,7},{7,3},{6,5},{5,6},{4,8},{8,4},{9,10},{10,9},{11,... | collective-permute-start | bytes 393224 | tf_op jit(solution)/shard_map/ppermute | solution.py:269
  25.8 2.7 %copy-start.1 = (bf16[3,3,256,256]{3,2,1,0:T(8,128)(2,1)S(1)}, bf16[3,3,256,256]{3,2,1,0:T(8,128)(2,1)}, u32[]{:S(2)}) copy-start(bf16[3,3,256,256]{3,2,1,0:T(8,128)(2,1)} %param.15) | copy-start | bytes 3538948
  25.8 2.7 %copy-start.3 = (bf16[256,256]{1,0:T(8,128)(2,1)S(1)}, bf16[256,256]{1,0:T(8,128)(2,1)}, u32[]{:S(2)}) copy-start(bf16[256,256]{1,0:T(8,128)(2,1)} %refs_12_.1) | copy-start | bytes 393220
  25.8 2.7 %copy-start.4 = (bf16[256,64]{0,1:T(8,128)(2,1)S(1)}, bf16[256,64]{0,1:T(8,128)(2,1)}, u32[]{:S(2)}) copy-start(bf16[256,64]{0,1:T(8,128)(2,1)} %param.18) | copy-start | bytes 98308
  25.8 2.7 %copy-start.6 = (s32[8,4]{0,1:T(4,128)S(1)}, s32[8,4]{0,1:T(4,128)}, u32[]{:S(2)}) copy-start(s32[8,4]{0,1:T(4,128)} %param.22) | copy-start | bytes 388
  25.8 2.7 %copy-start.11 = (f32[256]{0:T(256)S(1)}, f32[256]{0:T(256)}, u32[]{:S(2)}) copy-start(f32[256]{0:T(256)} %param.16) | copy-start | bytes 3076
  28.5 21.1 %copy-start.8 = (s32[8,4]{0,1:T(4,128)S(1)}, s32[8,4]{0,1:T(4,128)}, u32[]{:S(2)}) copy-start(s32[8,4]{0,1:T(4,128)} %param.21) | copy-start | bytes 388
  35.5 3.9 %collective-permute-start.4 = (bf16[8,32,256]{2,1,0:T(8,128)(2,1)S(1)}, bf16[8,32,256]{2,1,0:T(8,128)(2,1)S(1)}, u32[]{:S(2)}, u32[]{:S(2)}) collective-permute-start(bf16[8,32,256]{2,1,0:T(8,128)(2,1)S(1)} %get-tuple-element.22), channel_id=1, source_target_pairs={{0,1},{1,2},{2,3},{3,0},{4,5},{5,6},{6,7},{7,4},{8,9},{9,10},{10,1... | collective-permute-start | bytes 393224 | tf_op jit(solution)/shard_map/ppermute | solution.py:254
  36.6 10.5 %collective-permute-start.5 = (bf16[8,32,256]{2,1,0:T(8,128)(2,1)S(1)}, bf16[8,32,256]{2,1,0:T(8,128)(2,1)S(1)}, u32[]{:S(2)}, u32[]{:S(2)}) collective-permute-start(bf16[8,32,256]{2,1,0:T(8,128)(2,1)S(1)} %get-tuple-element.23), channel_id=1, source_target_pairs={{0,2},{1,3},{2,0},{3,1},{4,6},{5,7},{6,4},{7,5},{8,10},{9,11},{10,... | collective-permute-start | bytes 393224 | tf_op jit(solution)/shard_map/ppermute | solution.py:254
  37.4 12.2 %collective-permute-start.6 = (bf16[8,32,256]{2,1,0:T(8,128)(2,1)S(1)}, bf16[8,32,256]{2,1,0:T(8,128)(2,1)S(1)}, u32[]{:S(2)}, u32[]{:S(2)}) collective-permute-start(bf16[8,32,256]{2,1,0:T(8,128)(2,1)S(1)} %get-tuple-element.24), channel_id=1, source_target_pairs={{0,3},{1,0},{2,1},{3,2},{4,7},{5,4},{6,5},{7,6},{8,11},{9,8},{10,9... | collective-permute-start | bytes 393224 | tf_op jit(solution)/shard_map/ppermute | solution.py:254

commit v3 on v2

--- a/solution.py
+++ b/solution.py
@@ -68,14 +68,13 @@
 
 
 def send_kernel(n, rows, rotation, fields, *rest):
-    slabs = rest[:n]
-    staged, upright = rest[n:]
+    slabs, staged, upright = rest
     band = lax.axis_index("lat")
     me = lax.axis_index("lon")
     turn((4 - rotation[me, band]) % 4, staged, fields, upright)
-    for d in range(n):
-        group = group_of(band, lax.rem(me + d, n), n)
-        slabs[d][...] = upright[pl.ds(first_held(group, rows), rows + HALO)]
+    for s in range(n):
+        group = group_of(band, s, n)
+        slabs[s] = upright[pl.ds(first_held(group, rows), rows + HALO)]
 
 
 def columns_of(segment, size):
@@ -83,15 +82,13 @@
 
 
 def gather_kernel(n, rows, owner, *rest):
-    slabs = rest[:n]
-    grid, edge = rest[n:]
+    slabs, grid, edge = rest
     band = lax.axis_index("lat")
     me = lax.axis_index("lon")
     group = group_of(band, me, n)
-    size = slabs[0].shape[1]
-    for d in range(n):
-        source = lax.rem(me + n - d, n)
-        grid[:, columns_of(owner[source, band], size)] = slabs[d][...]
+    size = slabs.shape[2]
+    for s in range(n):
+        grid[:, columns_of(owner[s, band], size)] = slabs[s]
     edge[...] = grid[pl.ds(rows * (group % 2), HALO)]
 
 
@@ -137,8 +134,7 @@
 def rows_kernel(n, rows, size, owner, counts, *rest):
     grid, acts, sent, received = rest[:4]
     w_conv1, b_conv1, w_conv2, b_conv2, w_qv, w_key, w_out = rest[4:11]
-    results = rest[11 : n + 11]
-    taps1, taps2, mixed, attended = rest[n + 11 :]
+    results, taps1, taps2, mixed, attended = rest[11:]
     band = lax.axis_index("lat")
     me = lax.axis_index("lon")
     group = group_of(band, me, n)
@@ -191,20 +187,19 @@
         at = slice(r * cols, (r + 1) * cols)
         live = cell < counts[first_row + r]
         mixed[at, :] = (mixed[at, :].astype(jnp.float32) + jnp.where(live, update[at], 0.0)).astype(jnp.bfloat16)
-    for d in range(n):
-        segment = owner[lax.rem(me + d, n), band]
+    for s in range(n):
+        segment = owner[s, band]
         for r in range(rows):
-            results[d][r] = mixed[columns_of(segment + r * n, size), :]
+            results[s, r] = mixed[columns_of(segment + r * n, size), :]
 
 
 def store_kernel(n, rows, rotation, *rest):
-    slabs = rest[:n]
-    out, staged, upright = rest[n:]
-    band = lax.axis_index("lat")
-    me = lax.axis_index("lon")
-    for d in range(n):
-        group = group_of(band, lax.rem(me + n - d, n), n)
-        upright[pl.ds(group * rows, rows)] = slabs[d][...]
+    slabs, out, staged, upright = rest
+    band = lax.axis_index("lat")
+    me = lax.axis_index("lon")
+    for s in range(n):
+        group = group_of(band, s, n)
+        upright[pl.ds(group * rows, rows)] = slabs[s]
     turn(rotation[me, band] % 4, staged, upright, out)
 
 
@@ -250,8 +245,7 @@
         return jax.ShapeDtypeStruct(shape, bf16)
 
     def around(parts):
-        pairs = [[(i, (i + d) % n) for i in range(n)] for d in range(n)]
-        return [parts[0]] + [lax.ppermute(parts[d], "lon", pairs[d]) for d in range(1, n)]
+        return lax.all_to_all(parts, "lon", 0, 0)
 
     rotation, owner = rotation.T, owner.T
     w_first = w_conv1.reshape(3, 3 * chans, chans)
@@ -260,10 +254,10 @@
     b_second = b_conv2.reshape(1, chans)
     w_qv = jnp.concatenate([w_query.T, w_value.T], axis=0)
 
-    slabs = [array(rows + HALO, size, chans)] * n
+    slabs = array(n, rows + HALO, size, chans)
     slabs = around(call(send_kernel, "send", slabs, [rotation], [fields], [staging, block]))
     held = [array(rows + HALO, cols, chans), array(HALO, cols, chans)]
-    grid, sent = call(gather_kernel, "gather", held, [owner], slabs, [])
+    grid, sent = call(gather_kernel, "gather", held, [owner], [slabs], [])
     snake = [a * n + shard_of(a, g, n) for a in range(bands) for g in range(n)]
     pairs = [(snake[i], snake[i + 1 if i % 2 else i - 1]) for i in range(1, bands * n - 1)]
     received = lax.ppermute(sent, ("lat", "lon"), pairs)
@@ -278,7 +272,7 @@
     results = call(
         lambda n, rows, *refs: rows_kernel(n, rows, size, *refs),
         "rows",
-        [array(rows, size, chans)] * n,
+        array(n, rows, size, chans),
         [owner, counts],
         [grid, acts, sent, received, w_first, b_first, w_second, b_second, w_qv, w_key.T, w_out],
         [
@@ -289,7 +283,7 @@
         ],
     )
     results = around(results)
-    return call(store_kernel, "store", array(*fields.shape), [rotation], results, [staging, block])
+    return call(store_kernel, "store", array(*fields.shape), [rotation], [results], [staging, block])
 
 
 def solution(mesh):

time: 51.8 us -> 59.6 us (1.15)
  the two profiles are of different devices: /device:TPU:11 before, /device:TPU:0 now
where the time goes in v3:
time: 59.6 us; the launch traced here: 59.3 us
  blocking collectives  44 us (74%)
  Pallas kernels  12.5 us (21%)
  local copies, waits for them, and re-layouts  1.89 us (3%)
  starting transfers between devices  0.67 us (1%)
    all_to_all x2, blocking collectives, around(): return lax.all_to_all(parts, 'lon', 0, 0)  44 us
    pallas_call x5, Pallas kernels, call(): pl.pallas_call(functools.partial(kernel, n, rows), out_shape=out, in_spec...  12.5 us
    unnamed x27, local copies, waits for them, and re-layouts  1.89 us
  transfers between devices with their start and end apart: 1, of which 0 were waited for; matrix products, arithmetic and copies ran while one was open for 0% of the time, Pallas kernels for 4%

profile of v3, /device:TPU:0, one launch (start us, length us, event | category | flops | bytes accessed | tf_op | source)
XLA Modules:
  0.0 59.3 jit_solution(18018566704884986169)
XLA Ops:
  0.0 1.0 %copy-done.2 = bf16[32,32,256]{2,1,0:T(8,128)(2,1)S(1)} copy-done((bf16[32,32,256]{2,1,0:T(8,128)(2,1)S(1)}, bf16[32,32,256]{2,1,0:T(8,128)(2,1)}, u32[]{:S(2)}) %copy-start.2) | copy-done | bytes 524312
  1.0 0.7 %copy-done.6 = s32[8,4]{0,1:T(4,128)S(1)} copy-done((s32[8,4]{0,1:T(4,128)S(1)}, s32[8,4]{0,1:T(4,128)}, u32[]{:S(2)}) %copy-start.6) | copy-done | bytes 152
  1.7 1.0 %send.1 = bf16[4,10,32,256]{3,2,1,0:T(8,128)(2,1)S(1)} custom-call(s32[4,8]{1,0:T(4,128)S(1)} %bitcast.15, bf16[32,32,256]{2,1,0:T(8,128)(2,1)S(1)} %copy-done.2), custom_call_target="tpu_custom_call" | custom-call | tf_op jit(solution)/shard_map/send/pallas_call | solution.py:234
  2.7 0.0 copy-start.11
  2.7 0.0 copy-start.12
  2.7 0.0 copy-start
  2.7 0.0 copy-start.8
  2.7 0.0 copy-start.9
  2.7 23.9 %all_to_all.10.rest_0_ = bf16[4,10,32,256]{3,2,1,0:T(8,128)(2,1)S(1)} all-to-all(bf16[4,10,32,256]{3,2,1,0:T(8,128)(2,1)S(1)} %send.1), channel_id=1, replica_groups=mesh['lat'=8,'lon'=4] {'lon'}, dimensions={0} | all-to-all | bytes 1310720 | tf_op jit(solution)/shard_map/all_to_all | solution.py:248
  26.7 0.0 copy-done.5
  26.7 0.6 %gather.1 = (bf16[10,128,256]{2,1,0:T(8,128)(2,1)S(1)}, bf16[2,128,256]{2,1,0:T(8,128)(2,1)S(1)}) custom-call(s32[4,8]{1,0:T(4,128)S(1)} %bitcast.13, bf16[4,10,32,256]{3,2,1,0:T(8,128)(2,1)S(1)} %all_to_all.10.rest_0_), custom_call_target="tpu_custom_call" | custom-call | tf_op jit(solution)/shard_map/gather/pallas_call | solution.py:234
  27.3 0.7 %collective-permute-start = (bf16[2,128,256]{2,1,0:T(8,128)(2,1)S(1)}, bf16[2,128,256]{2,1,0:T(8,128)(2,1)S(1)}, u32[]{:S(2)}, u32[]{:S(2)}) collective-permute-start(bf16[2,128,256]{2,1,0:T(8,128)(2,1)S(1)} %get-tuple-element.8.refs_4_), channel_id=1, source_target_pairs={{1,2},{2,1},{3,7},{7,3},{6,5},{5,6},{4,8},{8,4},{9,10},{10,9},{11,... | collective-permute-start | bytes 393224 | tf_op jit(solution)/shard_map/ppermute | solution.py:263
  28.0 0.1 copy.13
  28.2 0.0 copy-start.1
  28.2 0.0 copy-start.3
  28.2 0.0 copy-start.4
  28.2 0.0 copy-start.10
  28.2 2.2 %first.1.refs_3_ = bf16[8,128,768]{2,1,0:T(8,128)(2,1)S(1)} custom-call(s32[256]{0:T(256)S(1)} %copy-done.8, bf16[10,128,256]{2,1,0:T(8,128)(2,1)S(1)} %get-tuple-element.7.refs_1_.refs_2_, bf16[3,768,256]{2,1,0:T(8,128)(2,1)S(1)} %bitcast.9, f32[1,256]{1,0:T(1,128)S(1)} %bitcast.17), custom_call_target="tpu_custom_call" | custom-call | tf_op jit(solution)/shard_map/first/pallas_call | solution.py:234
  30.4 0.0 collective-permute-done.refs_5_
  30.5 0.0 copy-done.1
  30.5 0.0 copy-start.7
  30.5 7.0 %rows.1 = bf16[4,8,32,256]{3,2,1,0:T(8,128)(2,1)S(1)} custom-call(s32[4,8]{1,0:T(4,128)S(1)} %bitcast.14, s32[256]{0:T(256)S(1)} %copy-done.8, bf16[10,128,256]{2,1,0:T(8,128)(2,1)S(1)} %get-tuple-element.7.refs_1_.refs_2_, bf16[8,128,768]{2,1,0:T(8,128)(2,1)S(1)} %first.1.refs_3_, bf16[2,128,256]{2,1,0:T(8,128)(2,1)S(1)} %get-tuple-element.8.refs_4_, ...), custom_call_target="tpu_custom_call" | custom-call | tf_op jit(solution)/shard_map/rows/pallas_call | solution.py:234
  37.5 20.1 %all_to_all.11.rest_0_ = bf16[4,8,32,256]{3,2,1,0:T(8,128)(2,1)S(1)} all-to-all(bf16[4,8,32,256]{3,2,1,0:T(8,128)(2,1)S(1)} %rows.1), channel_id=1, replica_groups=mesh['lat'=8,'lon'=4] {'lon'}, dimensions={0} | all-to-all | bytes 1048576 | tf_op jit(solution)/shard_map/all_to_all | solution.py:248
  57.5 1.7 %store.1 = bf16[32,32,256]{2,1,0:T(8,128)(2,1)} custom-call(s32[4,8]{1,0:T(4,128)S(1)} %bitcast.16, bf16[4,8,32,256]{3,2,1,0:T(8,128)(2,1)S(1)} %all_to_all.11.rest_0_), custom_call_target="tpu_custom_call" | custom-call | tf_op jit(solution)/shard_map/store/pallas_call | solution.py:234
  (13 shorter events, 0.0 us)
Async XLA Ops:
  0.0 1.0 %copy-start.2 = (bf16[32,32,256]{2,1,0:T(8,128)(2,1)S(1)}, bf16[32,32,256]{2,1,0:T(8,128)(2,1)}, u32[]{:S(2)}) copy-start(bf16[32,32,256]{2,1,0:T(8,128)(2,1)} %fields.1) | copy-start | bytes 1572868
  1.0 0.7 %copy-start.6 = (s32[8,4]{0,1:T(4,128)S(1)}, s32[8,4]{0,1:T(4,128)}, u32[]{:S(2)}) copy-start(s32[8,4]{0,1:T(4,128)} %param.21) | copy-start | bytes 388
  1.7 24.9 %copy-start.5 = (s32[8,4]{0,1:T(4,128)S(1)}, s32[8,4]{0,1:T(4,128)}, u32[]{:S(2)}) copy-start(s32[8,4]{0,1:T(4,128)} %param.22) | copy-start | bytes 388
  2.7 25.3 %copy-start.11 = (bf16[256,256]{1,0:T(8,128)(2,1)S(1)}, bf16[256,256]{1,0:T(8,128)(2,1)}, u32[]{:S(2)}) copy-start(bf16[256,256]{1,0:T(8,128)(2,1)} %param.17) | copy-start | bytes 393220
  2.7 25.4 %copy-start.12 = (bf16[256,64]{0,1:T(8,128)(2,1)S(1)}, bf16[256,64]{0,1:T(8,128)(2,1)}, u32[]{:S(2)}) copy-start(bf16[256,64]{0,1:T(8,128)(2,1)} %param.19) | copy-start | bytes 98308
  2.7 25.4 %copy-start = (bf16[3,3,256,256]{3,2,1,0:T(8,128)(2,1)S(1)}, bf16[3,3,256,256]{3,2,1,0:T(8,128)(2,1)}, u32[]{:S(2)}) copy-start(bf16[3,3,256,256]{3,2,1,0:T(8,128)(2,1)} %param.13) | copy-start | bytes 3538948
  2.7 25.4 %copy-start.8 = (s32[256]{0:T(256)S(1)}, s32[256]{0:T(256)}, u32[]{:S(2)}) copy-start(s32[256]{0:T(256)} %refs_1_.1) | copy-start | bytes 3076
  2.7 25.4 %copy-start.9 = (f32[256]{0:T(256)S(1)}, f32[256]{0:T(256)}, u32[]{:S(2)}) copy-start(f32[256]{0:T(256)} %param.14) | copy-start | bytes 3076
  27.3 3.1 %collective-permute-start = (bf16[2,128,256]{2,1,0:T(8,128)(2,1)S(1)}, bf16[2,128,256]{2,1,0:T(8,128)(2,1)S(1)}, u32[]{:S(2)}, u32[]{:S(2)}) collective-permute-start(bf16[2,128,256]{2,1,0:T(8,128)(2,1)S(1)} %get-tuple-element.8.refs_4_), channel_id=1, source_target_pairs={{1,2},{2,1},{3,7},{7,3},{6,5},{5,6},{4,8},{8,4},{9,10},{10,9},{11,... | collective-permute-start | bytes 393224 | tf_op jit(solution)/shard_map/ppermute | solution.py:263
  28.2 2.3 %copy-start.1 = (bf16[3,3,256,256]{3,2,1,0:T(8,128)(2,1)S(1)}, bf16[3,3,256,256]{3,2,1,0:T(8,128)(2,1)}, u32[]{:S(2)}) copy-start(bf16[3,3,256,256]{3,2,1,0:T(8,128)(2,1)} %param.15) | copy-start | bytes 3538948
  28.2 2.3 %copy-start.3 = (bf16[256,256]{1,0:T(8,128)(2,1)S(1)}, bf16[256,256]{1,0:T(8,128)(2,1)}, u32[]{:S(2)}) copy-start(bf16[256,256]{1,0:T(8,128)(2,1)} %refs_12_.1) | copy-start | bytes 393220
  28.2 2.3 %copy-start.4 = (bf16[256,64]{0,1:T(8,128)(2,1)S(1)}, bf16[256,64]{0,1:T(8,128)(2,1)}, u32[]{:S(2)}) copy-start(bf16[256,64]{0,1:T(8,128)(2,1)} %param.18) | copy-start | bytes 98308
  28.2 2.3 %copy-start.10 = (f32[256]{0:T(256)S(1)}, f32[256]{0:T(256)}, u32[]{:S(2)}) copy-start(f32[256]{0:T(256)} %param.16) | copy-start | bytes 3076
  30.5 27.1 %copy-start.7 = (s32[8,4]{0,1:T(4,128)S(1)}, s32[8,4]{0,1:T(4,128)}, u32[]{:S(2)}) copy-start(s32[8,4]{0,1:T(4,128)} %param.21) | copy-start | bytes 388

commit v4 on v2

v4 whole, which is shorter than its diff:
```python
import functools
import math

import jax
import jax.numpy as jnp
from jax import lax
from jax.experimental import pallas as pl
from jax.experimental.pallas import tpu as pltpu
from jax.sharding import PartitionSpec as P

HALO = 2
LANES = 128
GROUP = 256
VMEM_BYTES = 28 * 1024 * 1024


def group_of(band, shard, n):
    return jnp.where(band % 2 == 0, shard, n - 1 - shard)


def shard_of(band, group, n):
    return group if band % 2 == 0 else n - 1 - group


def first_held(group, rows):
    return group * rows - HALO * (group % 2)


def turn(quarter, staged, block, out, ready, done):
    size, _, chans = block.shape
    tiles = staged.shape[0]
    depth = GROUP // size
    pieces = size // depth

    def column(col):
        parts = [staged[t, pl.ds(col, size, stride=size), :] for t in range(tiles)]
        return jnp.concatenate(parts, axis=1).astype(jnp.bfloat16)

    def keep(i, row):
        for t in range(tiles):
            staged[t, pl.ds(i * size, size), :] = row[:, t * LANES : (t + 1) * LANES]

    @pl.when(quarter == 0)
    def _():
        for g in range(pieces):
            ready(g)
            out[g * depth : (g + 1) * depth] = block[g * depth : (g + 1) * depth]
            done(g)

    @pl.when(quarter == 1)
    def _():
        for i in range(size):
            if i % depth == 0:
                ready(i // depth)
            keep(i, block[i].astype(jnp.float32))
        for i in range(size):
            out[i] = column(size - 1 - i)
            if i % depth == depth - 1:
                done(i // depth)

    @pl.when(quarter == 2)
    def _():
        i = lax.broadcasted_iota(jnp.int32, (GROUP, GROUP), 0)
        j = lax.broadcasted_iota(jnp.int32, (GROUP, GROUP), 1)
        backwards = jnp.where(i + j == GROUP - 1, 1.0, 0.0).astype(jnp.bfloat16)
        for g in reversed(range(pieces)):
            ready(pieces - 1 - g)
            cells = block[size - (g + 1) * depth : size - g * depth].reshape(GROUP, chans)
            turned = jnp.dot(backwards, cells, preferred_element_type=jnp.float32).astype(jnp.bfloat16)
            out[g * depth : (g + 1) * depth] = turned.reshape(depth, size, chans)
            done(g)

    @pl.when(quarter == 3)
    def _():
        for i in range(size):
            if i % depth == 0:
                ready(i // depth)
            keep(size - 1 - i, block[i].astype(jnp.float32))
        for i in range(size):
            out[i] = column(i)
            if i % depth == depth - 1:
                done(i // depth)


def send_kernel(n, rows, rotation_in, fields, *rest):
    slabs = rest[:n]
    staged, block, upright, rotation, scalar_sem, sems = rest[n:]
    band = lax.axis_index("lat")
    me = lax.axis_index("lon")
    depth = GROUP // fields.shape[0]

    def piece(g):
        at = pl.ds(g * depth, depth)
        return pltpu.make_async_copy(fields.at[at], block.at[at], sems.at[g])

    scalars = pltpu.make_async_copy(rotation_in, rotation, scalar_sem)
    scalars.start()
    for g in range(fields.shape[0] // depth):
        piece(g).start()
    scalars.wait()
    turn((4 - rotation[me, band]) % 4, staged, block, upright, lambda g: piece(g).wait(), lambda g: None)
    for d in range(n):
        group = group_of(band, lax.rem(me + d, n), n)
        slabs[d][...] = upright[pl.ds(first_held(group, rows), rows + HALO)]


def load_kernel(n, rows, after, *refs):
    del after
    count = len(refs) // 2
    copies = [pltpu.make_async_copy(refs[i], refs[count + i], refs[-1].at[i]) for i in range(count)]
    for copy in copies:
        copy.start()
    for copy in copies:
        copy.wait()


def columns_of(segment, size):
    return pl.ds(pl.multiple_of(segment * size, size), size)


def gather_kernel(n, rows, owner, *rest):
    slabs = rest[:n]
    grid, edge = rest[n:]
    band = lax.axis_index("lat")
    me = lax.axis_index("lon")
    group = group_of(band, me, n)
    size = slabs[0].shape[1]
    for d in range(n):
        source = lax.rem(me + n - d, n)
        grid[:, columns_of(owner[source, band], size)] = slabs[d][...]
    edge[...] = grid[pl.ds(rows * (group % 2), HALO)]


def spread(taps, r, row):
    cols, chans = row.shape
    taps[r, :, :chans] = pltpu.roll(row, 1, 0).astype(jnp.bfloat16)
    taps[r, :, chans : 2 * chans] = row.astype(jnp.bfloat16)
    taps[r, :, 2 * chans :] = pltpu.roll(row, cols - 1, 0).astype(jnp.bfloat16)


def convolve(taps, weight, bias, count):
    cols, width = taps.shape[1:]
    total = bias[...]
    for i in range(3):
        window = taps[i : i + count].reshape(count * cols, width)
        total = total + jnp.dot(window, weight[i], preferred_element_type=jnp.float32)
    return total


def silu(x):
    return x / (1.0 + jnp.exp(-x))


def live_count(counts, row):
    inside = (row >= 0) & (row < counts.shape[0])
    return jnp.where(inside, counts[jnp.clip(row, 0, counts.shape[0] - 1)], 0)


def finish(n, count, first_row, grid_row, second, counts, owner, w_query, w_key, w_value, w_out, results, mixed, attended):
    band = lax.axis_index("lat")
    me = lax.axis_index("lon")
    chans = mixed.shape[1]
    cols = mixed.shape[0] // count
    head_dim = w_key.shape[0]
    heads = chans // head_dim
    cell = lax.broadcasted_iota(jnp.int32, (cols, chans), 0)
    for r in range(count):
        live = cell < counts[first_row + r]
        part = jnp.where(live, grid_row(r).astype(jnp.float32) + second[r * cols : (r + 1) * cols], 0.0)
        mixed[r * cols : (r + 1) * cols, :] = part.astype(jnp.bfloat16)
    flat = mixed[...].astype(jnp.float32)
    normed = (flat * lax.rsqrt(jnp.mean(flat * flat, axis=1, keepdims=True) + 1e-06)).astype(jnp.bfloat16)

    def by_last(a, b):
        return lax.dot_general(a, b, (((1,), (1,)), ((), ())), preferred_element_type=jnp.float32)

    keys = by_last(normed, w_key[...]).astype(jnp.bfloat16)
    query = by_last(w_query[...].T, normed).astype(jnp.bfloat16)
    value = by_last(w_value[...], normed).astype(jnp.bfloat16)
    key_at = lax.broadcasted_iota(jnp.int32, (cols, cols), 0)
    scale = math.log2(math.e) / head_dim**0.5
    for r in range(count):
        at = slice(r * cols, (r + 1) * cols)
        queries = jnp.concatenate([query[h * head_dim : (h + 1) * head_dim, at] for h in range(heads)], axis=1)
        scores = jnp.dot(keys[at], queries, preferred_element_type=jnp.float32)
        live = key_at < counts[first_row + r]
        expo = []
        totals = []
        for h in range(heads):
            part = jnp.where(live, scores[:, h * cols : (h + 1) * cols], -jnp.inf)
            part = jnp.exp2((part - jnp.max(part, axis=0, keepdims=True)) * scale)
            totals.append(jnp.sum(part, axis=0, keepdims=True))
            expo.append(part.astype(jnp.bfloat16))
        summed = jnp.dot(value[:, at], jnp.concatenate(expo, axis=1), preferred_element_type=jnp.float32)
        for h in range(heads):
            share = summed[:, h * cols : (h + 1) * cols] / totals[h]
            attended[h * head_dim : (h + 1) * head_dim, at] = share.astype(jnp.bfloat16)
    update = lax.dot_general(attended[...], w_out[...], (((0,), (0,)), ((), ())), preferred_element_type=jnp.float32)
    for r in range(count):
        at = slice(r * cols, (r + 1) * cols)
        live = cell < counts[first_row + r]
        mixed[at, :] = (mixed[at, :].astype(jnp.float32) + jnp.where(live, update[at], 0.0)).astype(jnp.bfloat16)
    for d in range(n):
        segment = owner[lax.rem(me + d, n), band]
        for r in range(count):
            results[d][r] = mixed[columns_of(segment + r * n, results[d].shape[1]), :]


def inner_kernel(n, rows, owner, counts, *rest):
    grid, w_conv1, b_conv1, w_conv2, b_conv2 = rest[:5]
    weights = rest[5:9]
    inner = rows - HALO
    edge_acts, results = rest[9], rest[10 : 10 + (n if inner else 0)]
    taps, acts, mixed, attended = rest[10 + len(results) :]
    band = lax.axis_index("lat")
    group = group_of(band, lax.axis_index("lon"), n)
    cols, chans = grid.shape[1:]
    cell = lax.broadcasted_iota(jnp.int32, (cols, chans), 0)
    top = band * (rows * n) + first_held(group, rows)
    for r in range(rows + HALO):
        spread(taps, r, grid[r].astype(jnp.float32))
    act = silu(convolve(taps, w_conv1, b_conv1, rows))
    for r in range(rows):
        live = cell < live_count(counts, top + 1 + r)
        spread(acts, r, jnp.where(live, act[r * cols : (r + 1) * cols], 0.0))
    edge_acts[...] = acts[pl.ds(inner * (group % 2), HALO)]
    if inner:
        second = convolve(acts, w_conv2, b_conv2, inner)
        finish(
            n, inner, top + 2, lambda r: grid[r + 2], second, counts, owner, *weights, results, mixed, attended
        )


def edge_kernel(n, rows, owner, counts, *rest):
    sent, received, edge_acts, w_conv1, b_conv1, w_conv2, b_conv2 = rest[:7]
    weights, results = rest[7:11], rest[11 : 11 + n]
    taps, acts, mixed, attended = rest[11 + n :]
    band = lax.axis_index("lat")
    group = group_of(band, lax.axis_index("lon"), n)
    odd = group % 2
    cols, chans = sent.shape[1:]
    cell = lax.broadcasted_iota(jnp.int32, (cols, chans), 0)
    first_row = band * (rows * n) + group * rows + (rows - HALO) * odd
    near, far = HALO * (1 - odd), HALO * odd
    for r in range(HALO):
        spread(taps, near + r, sent[r].astype(jnp.float32))
        spread(taps, far + r, received[r].astype(jnp.float32))
    act = silu(convolve(taps, w_conv1, b_conv1, HALO))
    acts[pl.ds(near, HALO)] = edge_acts[...]
    for r in range(HALO):
        live = cell < live_count(counts, first_row - 1 + far + r)
        spread(acts, far + r, jnp.where(live, act[r * cols : (r + 1) * cols], 0.0))
    second = convolve(acts, w_conv2, b_conv2, HALO)
    finish(n, HALO, first_row, lambda r: sent[r], second, counts, owner, *weights, results, mixed, attended)


def store_kernel(n, rows, rotation, *rest):
    inner = rows - HALO
    slabs = rest[: n if inner else 0]
    edges = rest[len(slabs) : len(slabs) + n]
    out, staged, upright, turned, sems = rest[len(slabs) + n :]
    band = lax.axis_index("lat")
    me = lax.axis_index("lon")
    depth = GROUP // out.shape[0]
    pieces = out.shape[0] // depth
    for d in range(n):
        group = group_of(band, lax.rem(me + n - d, n), n)
        odd = group % 2
        if inner:
            upright[pl.ds(group * rows + HALO * (1 - odd), inner)] = slabs[d][...]
        upright[pl.ds(group * rows + inner * odd, HALO)] = edges[d][...]

    def piece(g):
        at = pl.ds(g * depth, depth)
        return pltpu.make_async_copy(turned.at[at], out.at[at], sems.at[g])

    turn(rotation[me, band] % 4, staged, upright, turned, lambda g: None, lambda g: piece(g).start())
    for g in range(pieces):
        piece(g).wait()


def on_device(
    bands,
    n,
    fields,
    w_conv1,
    b_conv1,
    w_conv2,
    b_conv2,
    w_query,
    w_key,
    w_value,
    w_out,
    rotation,
    owner,
    counts,
):
    size, _, chans = fields.shape
    rows = size // n
    inner = rows - HALO
    cols = size * n
    bf16 = jnp.bfloat16
    smem = pl.BlockSpec(memory_space=pltpu.SMEM)
    vmem = pl.BlockSpec(memory_space=pltpu.VMEM)
    hbm = pl.BlockSpec(memory_space=pltpu.HBM)
    params = pltpu.CompilerParams(vmem_limit_bytes=VMEM_BYTES)
    pieces = size * size // GROUP

    def call(kernel, name, out, scalars, arrays, scratch, array_spec=vmem, scalar_spec=smem, out_spec=vmem):
        many = isinstance(out, list)
        return pl.pallas_call(
            functools.partial(kernel, n, rows),
            out_shape=out,
            in_specs=[scalar_spec] * len(scalars) + [array_spec] * len(arrays),
            out_specs=[out_spec] * len(out) if many else out_spec,
            scratch_shapes=scratch,
            compiler_params=params,
            name=name,
        )(*scalars, *arrays)

    def array(*shape):
        return jax.ShapeDtypeStruct(shape, bf16)

    def around(parts):
        pairs = [[(i, (i + d) % n) for i in range(n)] for d in range(n)]
        return [parts[0]] + [lax.ppermute(parts[d], "lon", pairs[d]) for d in range(1, n)]

    def in_hbm(x):
        return pltpu.with_memory_space_constraint(x, pltpu.HBM)

    loaded = [rotation.T, owner.T, counts]
    loaded += [w_conv1.reshape(3, 3 * chans, chans), b_conv1.reshape(1, chans)]
    loaded += [w_conv2.reshape(3, 3 * chans, chans), b_conv2.reshape(1, chans)]
    loaded = [in_hbm(x) for x in loaded + [w_query, w_key.T, w_value.T, w_out]]
    staging = pltpu.VMEM((chans // LANES, size * size, LANES), jnp.float32)
    block = pltpu.VMEM((size, size, chans), bf16)

    slabs = [array(rows + HALO, size, chans)] * n
    scratch = [staging, block, block, pltpu.SMEM(rotation.T.shape, rotation.dtype)]
    scratch += [pltpu.SemaphoreType.DMA, pltpu.SemaphoreType.DMA((pieces,))]
    slabs = call(send_kernel, "send", slabs, loaded[:1], [in_hbm(fields)], scratch, hbm, hbm)
    held = [pltpu.VMEM(x.shape, x.dtype) for x in loaded]
    scratch = [pltpu.SemaphoreType.DMA((len(loaded),))]
    rotation, owner, counts, *weights = call(load_kernel, "load", held, slabs[:1], loaded, scratch, hbm, hbm)
    slabs = around(slabs)

    held = [array(rows + HALO, cols, chans), array(HALO, cols, chans)]
    grid, sent = call(gather_kernel, "gather", held, [owner], slabs, [])
    snake = [a * n + shard_of(a, g, n) for a in range(bands) for g in range(n)]
    pairs = [(snake[i], snake[i + 1 if i % 2 else i - 1]) for i in range(1, bands * n - 1)]
    received = lax.ppermute(sent, ("lat", "lon"), pairs)

    def taps(count):
        return pltpu.VMEM((count, cols, 3 * chans), bf16)

    def flat(count):
        return [pltpu.VMEM((max(count, 1) * cols, chans), bf16), pltpu.VMEM((chans, max(count, 1) * cols), bf16)]

    edge_acts, *results = call(
        inner_kernel,
        "inner",
        [array(HALO, cols, 3 * chans)] + [array(inner, size, chans)] * (n if inner else 0),
        [owner, counts],
        [grid] + weights,
        [taps(rows + HALO), taps(rows)] + flat(inner),
    )
    results = around(results) if inner else []
    edges = call(
        edge_kernel,
        "edge",
        [array(HALO, size, chans)] * n,
        [owner, counts],
        [sent, received, edge_acts] + weights,
        [taps(2 * HALO), taps(2 * HALO)] + flat(HALO),
    )
    edges = around(edges)
    scratch = [staging, block, block, pltpu.SemaphoreType.DMA((pieces,))]
    return call(store_kernel, "store", array(*fields.shape), [rotation], results + edges, scratch, out_spec=hbm)


def solution(mesh):
    in_specs = (P("lat", "lon", None), P(), P(), P(), P(), P(), P(), P(), P(), P(), P(), P())
    out_specs = P("lat", "lon", None)
    body = functools.partial(on_device, mesh.shape["lat"], mesh.shape["lon"])
    return jax.shard_map(body, mesh=mesh, in_specs=in_specs, out_specs=out_specs, check_vma=False)
```

time: 51.8 us -> 47.5 us (0.917)
  the two profiles are of different devices: /device:TPU:11 before, /device:TPU:0 now
where the time goes in v4:
time: 47.5 us
  starting transfers between devices  21.3 us (45%)
  Pallas kernels  16.8 us (35%)
  waiting for transfers between devices  9.3 us (20%)
    ppermute x9, starting transfers between devices, around(): lax.ppermute(parts[d], 'lon', pairs[d])  20.6 us
    pallas_call x6, Pallas kernels, call(): pl.pallas_call(functools.partial(kernel, n, rows), out_shape=out, in_spec...  16.8 us
    ppermute x9, waiting for transfers between devices, around(): lax.ppermute(parts[d], 'lon', pairs[d])  9.3 us
  transfers between devices with their start and end apart: 10, of which 4 were waited for; matrix products, arithmetic and copies ran while one was open for 0% of the time, Pallas kernels for 26%

profile of v4, /device:TPU:0, one launch (start us, length us, event | category | flops | bytes accessed | tf_op | source)
XLA Modules:
  0.0 47.5 jit_solution(17258512108413801843)
XLA Ops:
  0.0 1.8 %send.1 = (bf16[10,32,256]{2,1,0:T(8,128)(2,1)S(1)}, bf16[10,32,256]{2,1,0:T(8,128)(2,1)S(1)}, bf16[10,32,256]{2,1,0:T(8,128)(2,1)S(1)}, bf16[10,32,256]{2,1,0:T(8,128)(2,1)S(1)}) custom-call(s32[4,8]{1,0:T(4,128)} %bitcast.12, bf16[32,32,256]{2,1,0:T(8,128)(2,1)} %fields.1), custom_call_target="tpu_custom_call" | custom-call | tf_op jit(solution)/shard_map/send/pallas_call | solution.py:311
  1.8 2.5 %collective-permute-start = (bf16[10,32,256]{2,1,0:T(8,128)(2,1)S(1)}, bf16[10,32,256]{2,1,0:T(8,128)(2,1)S(1)}, u32[]{:S(2)}, u32[]{:S(2)}) collective-permute-start(bf16[10,32,256]{2,1,0:T(8,128)(2,1)S(1)} %get-tuple-element.35), channel_id=1, source_target_pairs={{0,1},{1,2},{2,3},{3,0},{4,5},{5,6},{6,7},{7,4},{8,9},{9,10},{10,1... | collective-permute-start | bytes 491528 | tf_op jit(solution)/shard_map/ppermute | solution.py:326
  4.3 2.6 %collective-permute-start.1 = (bf16[10,32,256]{2,1,0:T(8,128)(2,1)S(1)}, bf16[10,32,256]{2,1,0:T(8,128)(2,1)S(1)}, u32[]{:S(2)}, u32[]{:S(2)}) collective-permute-start(bf16[10,32,256]{2,1,0:T(8,128)(2,1)S(1)} %get-tuple-element.36), channel_id=1, source_target_pairs={{0,2},{1,3},{2,0},{3,1},{4,6},{5,7},{6,4},{7,5},{8,10},{9,11},{10,... | collective-permute-start | bytes 491528 | tf_op jit(solution)/shard_map/ppermute | solution.py:326
  6.9 2.0 %collective-permute-start.2 = (bf16[10,32,256]{2,1,0:T(8,128)(2,1)S(1)}, bf16[10,32,256]{2,1,0:T(8,128)(2,1)S(1)}, u32[]{:S(2)}, u32[]{:S(2)}) collective-permute-start(bf16[10,32,256]{2,1,0:T(8,128)(2,1)S(1)} %get-tuple-element.37), channel_id=1, source_target_pairs={{0,3},{1,0},{2,1},{3,2},{4,7},{5,4},{6,5},{7,6},{8,11},{9,8},{10,9... | collective-permute-start | bytes 491528 | tf_op jit(solution)/shard_map/ppermute | solution.py:326
  8.9 1.8 %load.1 = (s32[4,8]{1,0:T(4,128)S(1)}, s32[4,8]{1,0:T(4,128)S(1)}, s32[256]{0:T(256)S(1)}, bf16[3,768,256]{2,1,0:T(8,128)(2,1)S(1)}, f32[1,256]{1,0:T(1,128)S(1)...) custom-call(bf16[10,32,256]{2,1,0:T(8,128)(2,1)S(1)} %get-tuple-elem, ...), custom_call_target="tpu_custom_call" | custom-call | tf_op jit(solution)/shard_map/load/pallas_call | solution.py:311
  10.7 0.7 %collective-permute-done.rest_1_ = bf16[10,32,256]{2,1,0:T(8,128)(2,1)S(1)} collective-permute-done((bf16[10,32,256]{2,1,0:T(8,128)(2,1)S(1)}, bf16[10,32,256]{2,1,0:T(8,128)(2,1)S(1)}, u32[]{:S(2)}, u32[]{:S(2)}) %collective-permute-start) | collective-permute-done | bytes 163872 | tf_op jit(solution)/shard_map/ppermute | solution.py:326
  11.4 6.2 %collective-permute-done.1.rest_2_ = bf16[10,32,256]{2,1,0:T(8,128)(2,1)S(1)} collective-permute-done((bf16[10,32,256]{2,1,0:T(8,128)(2,1)S(1)}, bf16[10,32,256]{2,1,0:T(8,128)(2,1)S(1)}, u32[]{:S(2)}, u32[]{:S(2)}) %collective-permute-start.1) | collective-permute-done | bytes 163872 | tf_op jit(solution)/shard_map/ppermute | solution.py:326
  17.6 0.6 %gather.1 = (bf16[10,128,256]{2,1,0:T(8,128)(2,1)S(1)}, bf16[2,128,256]{2,1,0:T(8,128)(2,1)S(1)}) custom-call(s32[4,8]{1,0:T(4,128)S(1)} %get-tuple-element.33.owner, bf16[10,32,256]{2,1,0:T(8,128)(2,1)S(1)} %get-tuple-element.31.after.rest_0_, bf16[10,32,256]{2,1,0:T(8,128)(2,1)S(1)} %collective-permute-done.rest_1_, ...), custom_call_target="tpu_custom_call" | custom-call | tf_op jit(solution)/shard_map/gather/pallas_call | solution.py:311
  18.2 0.7 %collective-permute-start.6 = (bf16[2,128,256]{2,1,0:T(8,128)(2,1)S(1)}, bf16[2,128,256]{2,1,0:T(8,128)(2,1)S(1)}, u32[]{:S(2)}, u32[]{:S(2)}) collective-permute-start(bf16[2,128,256]{2,1,0:T(8,128)(2,1)S(1)} %get-tuple-element.51.rest_0_), channel_id=1, source_target_pairs={{1,2},{2,1},{3,7},{7,3},{6,5},{5,6},{4,8},{8,4},{9,10},{10,9},{11,... | collective-permute-start | bytes 393224 | tf_op jit(solution)/shard_map/ppermute | solution.py:351
  18.9 7.3 %inner.1 = (bf16[2,128,768]{2,1,0:T(8,128)(2,1)S(1)}, bf16[6,32,256]{2,1,0:T(8,128)(2,1)S(1)}, bf16[6,32,256]{2,1,0:T(8,128)(2,1)S(1)}, bf16[6,32,256]{2,1,0:T(8,128)(2,1)S(1)}, bf16[6,32,256]{2,1,0:T(8,128)(2,1)S(1)}) custom-call(s32[4,8]{1,0:T(4,128)S(1)} %get-tuple-element.33.owner, s32[256]{0:T(256)S(1)} %get-tuple-element.34.counts, ...), custom_call_target="tpu_custom_call" | custom-call | tf_op jit(solution)/shard_map/inner/pallas_call | solution.py:311
  26.3 5.3 %collective-permute-start.3 = (bf16[6,32,256]{2,1,0:T(8,128)(2,1)S(1)}, bf16[6,32,256]{2,1,0:T(8,128)(2,1)S(1)}, u32[]{:S(2)}, u32[]{:S(2)}) collective-permute-start(bf16[6,32,256]{2,1,0:T(8,128)(2,1)S(1)} %get-tuple-element.48), channel_id=1, source_target_pairs={{0,1},{1,2},{2,3},{3,0},{4,5},{5,6},{6,7},{7,4},{8,9},{9,10},{10,1... | collective-permute-start | bytes 294920 | tf_op jit(solution)/shard_map/ppermute | solution.py:326
  31.6 2.3 %collective-permute-start.4 = (bf16[6,32,256]{2,1,0:T(8,128)(2,1)S(1)}, bf16[6,32,256]{2,1,0:T(8,128)(2,1)S(1)}, u32[]{:S(2)}, u32[]{:S(2)}) collective-permute-start(bf16[6,32,256]{2,1,0:T(8,128)(2,1)S(1)} %get-tuple-element.49), channel_id=1, source_target_pairs={{0,2},{1,3},{2,0},{3,1},{4,6},{5,7},{6,4},{7,5},{8,10},{9,11},{10,... | collective-permute-start | bytes 294920 | tf_op jit(solution)/shard_map/ppermute | solution.py:326
  33.9 2.0 %collective-permute-start.5 = (bf16[6,32,256]{2,1,0:T(8,128)(2,1)S(1)}, bf16[6,32,256]{2,1,0:T(8,128)(2,1)S(1)}, u32[]{:S(2)}, u32[]{:S(2)}) collective-permute-start(bf16[6,32,256]{2,1,0:T(8,128)(2,1)S(1)} %get-tuple-element.50), channel_id=1, source_target_pairs={{0,3},{1,0},{2,1},{3,2},{4,7},{5,4},{6,5},{7,6},{8,11},{9,8},{10,9... | collective-permute-start | bytes 294920 | tf_op jit(solution)/shard_map/ppermute | solution.py:326
  35.9 0.0 collective-permute-done.6.rest_1_
  35.9 3.2 %edge.1 = (bf16[2,32,256]{2,1,0:T(8,128)(2,1)S(1)}, bf16[2,32,256]{2,1,0:T(8,128)(2,1)S(1)}, bf16[2,32,256]{2,1,0:T(8,128)(2,1)S(1)}, bf16[2,32,256]{2,1,0:T(8,128)(2,1)S(1)}) custom-call(s32[4,8]{1,0:T(4,128)S(1)} %get-tuple-element.33.owner, s32[256]{0:T(256)S(1)} %get-tuple-element.34.counts, bf16[2,128,256]{2,1,0:T(8,128)(2,1)S(1)} %get-tuple-element.51.rest_0_, ...), custom_call_target="tpu_custom_call" | custom-call | tf_op jit(solution)/shard_map/edge/pallas_call | solution.py:311
  39.2 0.1 collective-permute-start.7
  39.2 0.6 %collective-permute-start.8 = (bf16[2,32,256]{2,1,0:T(8,128)(2,1)S(1)}, bf16[2,32,256]{2,1,0:T(8,128)(2,1)S(1)}, u32[]{:S(2)}, u32[]{:S(2)}) collective-permute-start(bf16[2,32,256]{2,1,0:T(8,128)(2,1)S(1)} %get-tuple-element.55), channel_id=1, source_target_pairs={{0,2},{1,3},{2,0},{3,1},{4,6},{5,7},{6,4},{7,5},{8,10},{9,11},{10,... | collective-permute-start | bytes 98312 | tf_op jit(solution)/shard_map/ppermute | solution.py:326
  39.8 0.0 collective-permute-done.3.rest_1_
  39.8 3.2 %collective-permute-start.9 = (bf16[2,32,256]{2,1,0:T(8,128)(2,1)S(1)}, bf16[2,32,256]{2,1,0:T(8,128)(2,1)S(1)}, u32[]{:S(2)}, u32[]{:S(2)}) collective-permute-start(bf16[2,32,256]{2,1,0:T(8,128)(2,1)S(1)} %get-tuple-element.56), channel_id=1, source_target_pairs={{0,3},{1,0},{2,1},{3,2},{4,7},{5,4},{6,5},{7,6},{8,11},{9,8},{10,9... | collective-permute-start | bytes 98312 | tf_op jit(solution)/shard_map/ppermute | solution.py:326
  43.0 0.0 collective-permute-done.4.rest_2_
  43.0 0.0 collective-permute-done.5.rest_3_
  43.0 2.0 %collective-permute-done.7.rest_5_ = bf16[2,32,256]{2,1,0:T(8,128)(2,1)S(1)} collective-permute-done((bf16[2,32,256]{2,1,0:T(8,128)(2,1)S(1)}, bf16[2,32,256]{2,1,0:T(8,128)(2,1)S(1)}, u32[]{:S(2)}, u32[]{:S(2)}) %collective-permute-start.7) | collective-permute-done | bytes 32800 | tf_op jit(solution)/shard_map/ppermute | solution.py:326
  45.0 0.5 collective-permute-done.9.rest_7_
  45.5 2.0 %store.1 = bf16[32,32,256]{2,1,0:T(8,128)(2,1)} custom-call(s32[4,8]{1,0:T(4,128)S(1)} %get-tuple-element.32.rotation, bf16[6,32,256]{2,1,0:T(8,128)(2,1)S(1)} %get-tuple-element.47.rest_0_, bf16[6,32,256]{2,1,0:T(8,128)(2,1)S(1)} %collective-permute-done.3.rest_1_, bf16[6,32,256]{2,1,0:T(8,128)(2,1)S(1)} %collective-permute-done.4.rest_2_, ...), custom_call_target="tpu_custom_call" | custom-call | tf_op jit(solution)/shard_map/store/pallas_call | solution.py:311
  (2 shorter events, 0.0 us)
Async XLA Ops:
  1.8 9.6 %collective-permute-start = (bf16[10,32,256]{2,1,0:T(8,128)(2,1)S(1)}, bf16[10,32,256]{2,1,0:T(8,128)(2,1)S(1)}, u32[]{:S(2)}, u32[]{:S(2)}) collective-permute-start(bf16[10,32,256]{2,1,0:T(8,128)(2,1)S(1)} %get-tuple-element.35), channel_id=1, source_target_pairs={{0,1},{1,2},{2,3},{3,0},{4,5},{5,6},{6,7},{7,4},{8,9},{9,10},{10,1... | collective-permute-start | bytes 491528 | tf_op jit(solution)/shard_map/ppermute | solution.py:326
  4.3 13.3 %collective-permute-start.1 = (bf16[10,32,256]{2,1,0:T(8,128)(2,1)S(1)}, bf16[10,32,256]{2,1,0:T(8,128)(2,1)S(1)}, u32[]{:S(2)}, u32[]{:S(2)}) collective-permute-start(bf16[10,32,256]{2,1,0:T(8,128)(2,1)S(1)} %get-tuple-element.36), channel_id=1, source_target_pairs={{0,2},{1,3},{2,0},{3,1},{4,6},{5,7},{6,4},{7,5},{8,10},{9,11},{10,... | collective-permute-start | bytes 491528 | tf_op jit(solution)/shard_map/ppermute | solution.py:326
  6.9 10.7 %collective-permute-start.2 = (bf16[10,32,256]{2,1,0:T(8,128)(2,1)S(1)}, bf16[10,32,256]{2,1,0:T(8,128)(2,1)S(1)}, u32[]{:S(2)}, u32[]{:S(2)}) collective-permute-start(bf16[10,32,256]{2,1,0:T(8,128)(2,1)S(1)} %get-tuple-element.37), channel_id=1, source_target_pairs={{0,3},{1,0},{2,1},{3,2},{4,7},{5,4},{6,5},{7,6},{8,11},{9,8},{10,9... | collective-permute-start | bytes 491528 | tf_op jit(solution)/shard_map/ppermute | solution.py:326
  18.2 17.7 %collective-permute-start.6 = (bf16[2,128,256]{2,1,0:T(8,128)(2,1)S(1)}, bf16[2,128,256]{2,1,0:T(8,128)(2,1)S(1)}, u32[]{:S(2)}, u32[]{:S(2)}) collective-permute-start(bf16[2,128,256]{2,1,0:T(8,128)(2,1)S(1)} %get-tuple-element.51.rest_0_), channel_id=1, source_target_pairs={{1,2},{2,1},{3,7},{7,3},{6,5},{5,6},{4,8},{8,4},{9,10},{10,9},{11,... | collective-permute-start | bytes 393224 | tf_op jit(solution)/shard_map/ppermute | solution.py:351
  26.3 13.5 %collective-permute-start.3 = (bf16[6,32,256]{2,1,0:T(8,128)(2,1)S(1)}, bf16[6,32,256]{2,1,0:T(8,128)(2,1)S(1)}, u32[]{:S(2)}, u32[]{:S(2)}) collective-permute-start(bf16[6,32,256]{2,1,0:T(8,128)(2,1)S(1)} %get-tuple-element.48), channel_id=1, source_target_pairs={{0,1},{1,2},{2,3},{3,0},{4,5},{5,6},{6,7},{7,4},{8,9},{9,10},{10,1... | collective-permute-start | bytes 294920 | tf_op jit(solution)/shard_map/ppermute | solution.py:326
  31.6 11.5 %collective-permute-start.4 = (bf16[6,32,256]{2,1,0:T(8,128)(2,1)S(1)}, bf16[6,32,256]{2,1,0:T(8,128)(2,1)S(1)}, u32[]{:S(2)}, u32[]{:S(2)}) collective-permute-start(bf16[6,32,256]{2,1,0:T(8,128)(2,1)S(1)} %get-tuple-element.49), channel_id=1, source_target_pairs={{0,2},{1,3},{2,0},{3,1},{4,6},{5,7},{6,4},{7,5},{8,10},{9,11},{10,... | collective-permute-start | bytes 294920 | tf_op jit(solution)/shard_map/ppermute | solution.py:326
  33.9 9.2 %collective-permute-start.5 = (bf16[6,32,256]{2,1,0:T(8,128)(2,1)S(1)}, bf16[6,32,256]{2,1,0:T(8,128)(2,1)S(1)}, u32[]{:S(2)}, u32[]{:S(2)}) collective-permute-start(bf16[6,32,256]{2,1,0:T(8,128)(2,1)S(1)} %get-tuple-element.50), channel_id=1, source_target_pairs={{0,3},{1,0},{2,1},{3,2},{4,7},{5,4},{6,5},{7,6},{8,11},{9,8},{10,9... | collective-permute-start | bytes 294920 | tf_op jit(solution)/shard_map/ppermute | solution.py:326
  39.2 5.9 %collective-permute-start.7 = (bf16[2,32,256]{2,1,0:T(8,128)(2,1)S(1)}, bf16[2,32,256]{2,1,0:T(8,128)(2,1)S(1)}, u32[]{:S(2)}, u32[]{:S(2)}) collective-permute-start(bf16[2,32,256]{2,1,0:T(8,128)(2,1)S(1)} %get-tuple-element.54), channel_id=1, source_target_pairs={{0,1},{1,2},{2,3},{3,0},{4,5},{5,6},{6,7},{7,4},{8,9},{9,10},{10,1... | collective-permute-start | bytes 98312 | tf_op jit(solution)/shard_map/ppermute | solution.py:326
  39.2 5.8 %collective-permute-start.8 = (bf16[2,32,256]{2,1,0:T(8,128)(2,1)S(1)}, bf16[2,32,256]{2,1,0:T(8,128)(2,1)S(1)}, u32[]{:S(2)}, u32[]{:S(2)}) collective-permute-start(bf16[2,32,256]{2,1,0:T(8,128)(2,1)S(1)} %get-tuple-element.55), channel_id=1, source_target_pairs={{0,2},{1,3},{2,0},{3,1},{4,6},{5,7},{6,4},{7,5},{8,10},{9,11},{10,... | collective-permute-start | bytes 98312 | tf_op jit(solution)/shard_map/ppermute | solution.py:326
  39.8 5.7 %collective-permute-start.9 = (bf16[2,32,256]{2,1,0:T(8,128)(2,1)S(1)}, bf16[2,32,256]{2,1,0:T(8,128)(2,1)S(1)}, u32[]{:S(2)}, u32[]{:S(2)}) collective-permute-start(bf16[2,32,256]{2,1,0:T(8,128)(2,1)S(1)} %get-tuple-element.56), channel_id=1, source_target_pairs={{0,3},{1,0},{2,1},{3,2},{4,7},{5,4},{6,5},{7,6},{8,11},{9,8},{10,9... | collective-permute-start | bytes 98312 | tf_op jit(solution)/shard_map/ppermute | solution.py:326
